TPU v7x, 256 devices: a whole 4x4x8 slice. The times are simulated.
256 devices in a mesh: section: 4 (over x), vocab: 64 (over z, y, core).
Axes of the slice: x: 4, y: 4, z: 8, core: 2. Of those that a mesh axis runs over, the one named last changes fastest.
Arguments:
- hidden: bfloat16 [4, 128, 8192], P('section', 'vocab'), may hold values from -240 to 240
- out_head: bfloat16 [8192, 65536], P('section', 'vocab'), may hold values from -1 to 1
- targets: int32 [4, 128], P('section'), may hold values from 0 to 65535
- scale_index: int32 [4], P('section'), may hold values from 0 to 7
Outputs:
- grad_head: bfloat16 [8192, 65536], P('section', 'vocab')
- grad_hidden: bfloat16 [4, 128, 8192], P('section', 'vocab')
- exit_loss: float32 [4], P('section')
All inputs are finite; a program needn't handle non-finite values.
Results may differ from a plain program's by a relative error of at most 0.0055.
Values may be sent and summed in bfloat16 or wider, within the bound.
A program may use at most 64 MiB of HBM per device.

v0:
```python
import jax
import jax.numpy as jnp
from jax import lax
from jax.sharding import PartitionSpec as P


def on_device(hidden, out_head, targets, scale_index):
    pieces = lax.all_to_all(hidden, "section", split_axis=2, concat_axis=0, tiled=True)
    gathered = lax.all_gather(pieces, "vocab", axis=1, tiled=True)
    partial_value = jnp.einsum(
        "srd,dv->srv", gathered, out_head, preferred_element_type=jnp.float32
    )
    logits = lax.psum_scatter(partial_value, "section", scatter_dimension=0, tiled=True)[0]
    width = out_head.shape[1]
    columns = lax.axis_index("vocab") * width + jnp.arange(width, dtype=jnp.int32)
    onehot = (targets[0][:, None] == columns[None, :]).astype(jnp.float32)
    local_target = jnp.sum(logits * onehot, axis=1)
    local_peak = jnp.max(logits, axis=1)
    peak = lax.pmax(local_peak, "vocab")
    local_total = jnp.sum(jnp.exp(logits - peak[:, None]), axis=1)
    total, target_logit = lax.psum((local_total, local_target), "vocab")
    lse = peak + jnp.log(total)
    exit_loss = jnp.mean(lse - target_logit).reshape(1)
    weight = 4.0 * (scale_index[0].astype(jnp.float32) + 1.0)
    exit_grad = (weight * (jnp.exp(logits - lse[:, None]) - onehot)).astype(jnp.bfloat16)
    every_grad = lax.all_gather(exit_grad[None], "section", axis=0, tiled=True)
    grad_head = jnp.einsum(
        "srd,srv->dv", gathered, every_grad, preferred_element_type=jnp.float32
    ).astype(jnp.bfloat16)
    grad_part = jnp.einsum("srv,dv->srd", every_grad, out_head, preferred_element_type=jnp.float32)
    regrouped = lax.all_to_all(grad_part, "section", split_axis=0, concat_axis=2, tiled=True)
    grad_hidden = lax.psum_scatter(regrouped, "vocab", scatter_dimension=1, tiled=True).astype(
        jnp.bfloat16
    )
    return (grad_head, grad_hidden, exit_loss)


def solution(mesh):
    in_specs = (
        P("section", "vocab", None),
        P("section", "vocab"),
        P("section", None),
        P("section"),
    )
    out_specs = (P("section", "vocab"), P("section", "vocab", None), P("section"))
    return jax.shard_map(
        on_device, mesh=mesh, in_specs=in_specs, out_specs=out_specs, check_vma=False
    )
```

profile of v0, /device:TPU:2, one launch (start us, length us, event | category | flops | bytes accessed | tf_op | source)
XLA Modules:
  0.0 967.2 jit_solution(7086552007081652349)
XLA Ops:
  7.2 0.0 all-gather.6.cloned.1.call-start
  7.2 8.2 copy.21
  15.4 0.5 broadcast.55
  15.9 45.2 %reduce.1 = bf16[8192,2]{1,0:T(8,128)(2,1)S(1)} reduce(bf16[8192,1,2]{2,1,0:T(2,128)(2,1)} %bitcast.40, bf16[]{:T(256)} %broadcast.55), dimensions={1}, to_apply=%bitcast.36.reduce_sub_computation | reduce | bytes 65538
  61.1 3.2 reshape.82
  64.4 8.6 all_to_all.36
  73.0 5.9 reshape.83
  78.9 8.1 copy.22
  87.0 0.7 all_to_all.27
  87.6 0.0 all-gather.6.cloned.1.call-update
  87.7 0.0 copy-start
  87.7 0.2 reduce-scatter.2.cloned.1.call-start
  87.9 79.2 %all-gather.6.cloned.1.call-done = bf16[4,1,128,2048]{3,0,1,2:T(4,128)(2,1)} async-done(((bf16[4,1,2,2048]{3,0,1,2:T(4,128)(2,1)}), bf16[4,1,128,2048]{3,0,1,2:T(4,128)(2,1)}) %all-gather.6.cloned.1.call-update) | async-done | bytes 2097168 | tf_op jit(solution)/shard_map/all_gather | solution.py:9
  167.1 7.9 fusion.2
  175.0 0.0 reduce-scatter.2.cloned.1.call-update
  175.1 0.0 all-gather.4.cloned.1.call-start
  175.8 28.1 %reduce-scatter.2.cloned.1.call-done = f32[1,128,1024]{2,1,0:T(8,128)} async-done(((f32[4,128,1024]{2,1,0:T(8,128)}), f32[1,128,1024]{2,1,0:T(8,128)}) %reduce-scatter.2.cloned.1.call-update) | async-done | bytes 524304 | tf_op jit(solution)/shard_map/reduce_scatter | solution.py:13
  203.9 1.2 reduce_max.9
  205.0 129.0 %pmax.7 = f32[128]{0:T(128)S(1)} all-reduce(f32[128]{0:T(128)S(1)} %reduce_max.9), channel_id=1, replica_groups=mesh['section'=4,'vocab'=64] {'vocab'}, use_global_device_ids=true, to_apply=%region_2.0 | all-reduce | flops 128 | bytes 1024 | tf_op jit(solution)/shard_map/pmax | solution.py:19
  334.1 0.0 copy-done
  334.1 1.3 fusion.11
  335.4 124.1 %psum.14 = f32[128]{0:T(128)S(1)} all-reduce(f32[128]{0:T(128)S(1)} %get-tuple-element.16), channel_id=1, replica_groups=mesh['section'=4,'vocab'=64] {'vocab'}, use_global_device_ids=true, to_apply=%region_4.0 | all-reduce | flops 128 | bytes 1024 | tf_op jit(solution)/shard_map/psum | solution.py:21
  459.4 2.0 multiply_convert_fusion
  461.4 0.0 all-gather.4.cloned.1.call-update
  461.4 21.5 %all-gather.4.cloned.1.call-done = bf16[4,128,1024]{2,1,0:T(8,128)(2,1)} async-done(((bf16[1,128,1024]{2,1,0:T(8,128)(2,1)}), bf16[4,128,1024]{2,1,0:T(8,128)(2,1)}) %all-gather.4.cloned.1.call-update) | async-done | bytes 1048592 | tf_op jit(solution)/shard_map/all_gather | solution.py:26
  482.9 6.9 fusion
  489.7 0.0 copy-start.3
  489.7 0.0 copy-start.1
  489.7 0.0 copy-start.2
  489.7 6.5 all-to-all-start.1
  496.3 0.0 copy-done.3
  496.3 0.6 dynamic-slice
  497.5 0.0 copy-done.1
  497.5 0.0 copy-done.2
  497.5 5.9 fusion.4
  503.4 6.4 copy.28
  509.8 33.3 %all-to-all-done.1 = f32[4,128,2048]{2,1,0:T(8,128)} async-done(((f32[4,128,2048]{2,1,0:T(8,128)}), f32[4,128,2048]{2,1,0:T(8,128)}, u32[]{:S(2)}, u32[]{:S(2)}) %all-to-all-start.1) | async-done | bytes 4194336 | tf_op jit(solution)/shard_map/all_to_all | solution.py:31
  543.1 5.3 copy.26
  548.4 9.6 copy.27
  558.1 398.6 %all-reduce.3 = (bf16[1,128,8192]{2,0,1:T(2,128)(2,1)}, f32[128]{0:T(128)S(1)}) all-reduce(f32[1,128,8192]{2,0,1:T(1,128)} %copy.27, f32[128]{0:T(128)S(1)} %get-tuple-element.15), channel_id=4, replica_groups=mesh['section'=4,'vocab'=64] {'vocab'}, use_global_device_ids=true, to_apply=%region_5.0.clone | all-reduce | flops 1048704 | bytes 6292480
  956.7 0.6 subtract_reduce_fusion
  957.3 0.9 dynamic-slice_convert_fusion
  958.2 0.7 copy.29
  (2 shorter events, 0.0 us)
Async XLA Ops:
  7.2 160.0 %all-gather.6.cloned.1.call-start = ((), (), s32[]{:S(2)}) async-start(), calls=%async_computation.5 | async-start | bytes 2129920 | tf_op jit(solution)/shard_map/all_gather | solution.py:9
  87.7 246.4 %copy-start = (s32[1,128]{1,0:T(1,128)S(1)}, s32[1,128]{1,0:T(1,128)}, u32[]{:S(2)}) copy-start(s32[1,128]{1,0:T(1,128)} %param.6) | copy-start | bytes 1540
  87.7 116.2 %reduce-scatter.2.cloned.1.call-start = ((), (), s32[]{:S(2)}) async-start(), calls=%async_computation.3 | async-start | bytes 2621440 | tf_op jit(solution)/shard_map/reduce_scatter | solution.py:13
  175.1 307.8 %all-gather.4.cloned.1.call-start = ((), (), s32[]{:S(2)}) async-start(), calls=%async_computation.4 | async-start | bytes 1310720 | tf_op jit(solution)/shard_map/all_gather | solution.py:26
  489.7 6.5 copy-start.3
  489.7 7.8 copy-start.1
  489.7 7.8 copy-start.2
  489.7 53.4 %all-to-all-start.1 = ((f32[4,128,2048]{2,1,0:T(8,128)}), f32[4,128,2048]{2,1,0:T(8,128)}, u32[]{:S(2)}, u32[]{:S(2)}) async-start(f32[4,128,2048]{2,1,0:T(8,128)} %fusion), calls=%async_computation.2 | async-start | bytes 8388608 | tf_op jit(solution)/shard_map/all_to_all | solution.py:31
Sparse Core Ops, SparseCore 0:
  87.8 79.2 all-gather.5
  175.2 28.6 reduce-scatter.1
  461.5 21.3 all-gather.3
where the time goes:
time: 969 us; the launch traced here: 967 us
  blocking collectives  660 us (68%)
  waiting for transfers between devices  162 us (17%)
  other arithmetic  50.2 us (5%)
  local copies, waits for them, and re-layouts  50.1 us (5%)
  matrix products  20.6 us (2%)
  between operations  16.9 us (2%)
    unnamed x1, blocking collectives  399 us
    pmax x1, blocking collectives, on_device(): peak = lax.pmax(local_peak, 'vocab')  129 us
    psum x1, blocking collectives, on_device(): total, target_logit = lax.psum((local_total, local_target), 'vocab')  124 us
    all_gather x1, waiting for transfers between devices, on_device(): gathered = lax.all_gather(pieces, 'vocab', axis=1, tiled=True)  79.2 us
    unnamed x1, other arithmetic  45.2 us
    all_to_all x1, waiting for transfers between devices, on_device(): lax.all_to_all(grad_part, 'section', split_axis=0, concat_axis=2, tiled=T...  33.3 us
    reduce_scatter x1, waiting for transfers between devices, on_device(): lax.psum_scatter(partial_value, 'section', scatter_dimension=0, tiled=True)  28.1 us
    unnamed x15, local copies, waits for them, and re-layouts  25.5 us
  transfers between devices with their start and end apart: 4, of which 4 were waited for; matrix products, arithmetic and copies ran while one was open for 1% of the time, Pallas kernels for 0%

commit v1 on v0

v1 whole, which is shorter than its diff:
```python
import functools

import jax
import jax.numpy as jnp
from jax import lax
from jax.experimental import pallas as pl
from jax.experimental.pallas import tpu as pltpu
from jax.sharding import PartitionSpec as P

MESH = pl.DeviceIdType.MESH
F32 = jnp.float32
BF16 = jnp.bfloat16

NX, NZ, NY = 4, 8, 4
LANES = 128
SUB = 16
FEAT = SUB * LANES
WIDTH = 1024
HALF = WIDTH // 2
GROUP = NY * NZ
CHUNK = NX * GROUP


def kernel(
    hid, w_hbm, tgt, scale, head_hbm, ghid, loss,
    w, head, hs32, hs, g, f, h, part, relay, final, u, grad,
    st_send, st_core, st_y, st_z, st_x,
    core_out, core_in, keep, y_out, y_in, zf, z_out, z_in, x_out, x_in,
    w_sem, head_sem,
    hx_s, hx_r, hz_s, hz_r, hy_s, hy_r, hc_s, hc_r,
    rl_s, rl_r, fn_s, fn_r, ux_s, ux_r,
    sc_s, sc_r, sy_s, sy_r, sz_s, sz_r, sx_s, sx_r,
    gc_s, gc_r, gy_s, gy_r, gz_s, gz_r, gx_s, gx_r,
):
    x = lax.axis_index("section")
    v = lax.axis_index("vocab")
    z, y, c = v // 8, (v // 2) % 4, v % 2
    oc = 1 - c

    def at(px, pz, py, pc):
        return (px, (pz * NY + py) * 2 + pc)

    def x_peer(d):
        return at((x + d) % NX, z, y, c)

    def y_peer(d):
        return at(x, z, (y + d) % NY, c)

    def z_peer(d):
        return at(x, (z + d) % NZ, y, c)

    core_peer = at(x, z, y, oc)
    sent = []

    def send(src, dst, s_sem, r_sem, peer):
        copy = pltpu.make_async_remote_copy(
            src_ref=src, dst_ref=dst, send_sem=s_sem, recv_sem=r_sem,
            device_id=peer, device_id_type=MESH,
        )
        copy.start()
        sent.append(copy)

    def got(ref, sem):
        pltpu.make_async_copy(ref, ref, sem).wait()

    barrier = pltpu.get_barrier_semaphore()
    peers = (
        [x_peer(d) for d in range(1, NX)]
        + [core_peer]
        + [y_peer(d) for d in range(1, NY)]
        + [z_peer(d) for d in range(1, NZ)]
    )
    for peer in peers:
        pl.semaphore_signal(barrier, inc=1, device_id=peer, device_id_type=MESH)

    w_copy = pltpu.make_async_copy(w_hbm, w, w_sem)
    w_copy.start()

    own = hid[0].astype(F32)
    for xx in range(NX):
        for k in range(SUB):
            at0 = xx * FEAT + k * LANES
            hs32[xx, :, k, :] = own[:, at0 : at0 + LANES]
    hs[...] = hs32[...].astype(BF16)

    place = lax.broadcasted_iota(jnp.int32, (128, 128), 0)
    row = lax.broadcasted_iota(jnp.int32, (128, 128), 1)
    pl_l, pl_c, pl_y, pl_z = place // 64, (place // 32) % 2, (place // 8) % 4, place % 8
    match = row == pl_z * 16 + pl_y * 4 + pl_c * 2 + pl_l
    tcol_all = jnp.sum(
        jnp.where(match, tgt[...].astype(F32), 0.0), axis=1, keepdims=True
    )
    eye = place == row
    trow_all = jnp.sum(jnp.where(eye, tcol_all, 0.0), axis=0, keepdims=True)
    st_x[x, 2:3, :] = trow_all
    st_send[0] = jnp.zeros((8, LANES), F32)

    pl.semaphore_wait(barrier, len(peers))

    for d in range(1, NX):
        send(hs.at[(x + d) % NX], g.at[:, c, x, y, z], hx_s.at[d - 1], hx_r.at[d - 1], x_peer(d))
    for l in range(2):
        g[l, c, x, y, z] = hs[x, l]
    for d in range(1, NX):
        got(hs.at[0], hx_r.at[d - 1])

    for l in range(2):
        for d in range(1, NZ):
            piece = g.at[l, c, :, y, z]
            send(piece, piece, hz_s.at[l, d - 1], hz_r.at[l, d - 1], z_peer(d))
    for l in range(2):
        for d in range(1, NZ):
            got(g.at[l, c, :, y, 0], hz_r.at[l, d - 1])
        block = g.at[l, c, :, y]
        for d in range(1, NY):
            send(block, block, hy_s.at[l, d - 1], hy_r.at[l, d - 1], y_peer(d))
        send(block, block, hc_s.at[l, 0], hc_r.at[l, 0], core_peer)

    def gathered_own(l):
        for d in range(1, NY):
            block = g.at[l, c, :, (y + NY - d) % NY]
            got(block, hy_r.at[l, d - 1])
            send(block, block, hc_s.at[l, d], hc_r.at[l, d], core_peer)

    def gathered_other(l):
        for d in range(NY):
            got(g.at[l, oc, :, 0], hc_r.at[l, d])

    def logits_part(l, cc, k):
        f[...] = g[l, cc].reshape(CHUNK * SUB, LANES).astype(F32)
        for j in range(SUB):
            h[l, cc, :, j * LANES : (j + 1) * LANES] = f[pl.ds(j, CHUNK, stride=SUB), :].astype(BF16)
        if k == 0:
            w_copy.wait()

        def tile(n, _):
            cols = pl.ds(pl.multiple_of(n * 256, 256), 256)
            out = jnp.dot(h[l, cc], w[:, cols], preferred_element_type=F32)
            part[k, :, :, cols] = out.reshape(NX, GROUP, 256)
            return 0

        lax.fori_loop(0, WIDTH // 256, tile, 0)
        far = part.at[k, (x + 2) % NX]
        send(far.at[:, pl.ds(0, HALF)], relay.at[k, 0], rl_s.at[k, 0], rl_r.at[k, 0], x_peer(1))
        send(far.at[:, pl.ds(HALF, HALF)], relay.at[k, 1], rl_s.at[k, 1], rl_r.at[k, 1], x_peer(3))

    def logits_relay(k):
        right, left = (x + 1) % NX, (x + 3) % NX
        got(relay.at[k, 0], rl_r.at[k, 0])
        part[k, right, :, :HALF] = part[k, right, :, :HALF] + relay[k, 0]
        send(part.at[k, right], final.at[k, 0], fn_s.at[k, 0], fn_r.at[k, 0], x_peer(1))
        got(relay.at[k, 1], rl_r.at[k, 1])
        part[k, left, :, HALF:] = part[k, left, :, HALF:] + relay[k, 1]
        send(part.at[k, left], final.at[k, 1], fn_s.at[k, 1], fn_r.at[k, 1], x_peer(3))

    columns = v * WIDTH + lax.broadcasted_iota(jnp.int32, (GROUP, WIDTH), 1)
    lane = lax.broadcasted_iota(jnp.int32, (GROUP, LANES), 1)
    sub = lax.broadcasted_iota(jnp.int32, (GROUP, LANES), 0)

    def first_lane(l, cc):
        return (l * 2 + cc) * GROUP

    def as_column(line, l, cc):
        here = lane == sub + first_lane(l, cc)
        return jnp.sum(jnp.where(here, line, 0.0), axis=1, keepdims=True)

    def softmax_part(l, cc, k):
        got(final.at[k, 0], fn_r.at[k, 0])
        got(final.at[k, 1], fn_r.at[k, 1])
        logits = part[k, x] + final[k, 0] + final[k, 1]
        peak = jnp.max(logits, axis=1, keepdims=True)
        raised = jnp.exp(logits - peak)
        total = jnp.sum(raised, axis=1, keepdims=True)
        target = as_column(trow_all, l, cc).astype(jnp.int32)
        hit = jnp.sum(jnp.where(columns == target, logits, 0.0), axis=1, keepdims=True)
        u[l, cc, x] = raised.astype(BF16)
        for d in range(1, NX):
            send(u.at[l, cc, x], u.at[l, cc, x], ux_s.at[k, d - 1], ux_r.at[k, d - 1], x_peer(d))
        here = lane == sub + first_lane(l, cc)
        for i, value in enumerate((peak, total, hit)):
            line = jnp.sum(jnp.where(here, value, 0.0), axis=0, keepdims=True)
            st_send[0, i : i + 1, :] = st_send[0, i : i + 1, :] + line

    order = [(0, c), (0, oc), (1, c), (1, oc)]
    gathered_own(0)
    logits_part(0, c, 0)
    gathered_other(0)
    logits_part(0, oc, 1)
    logits_relay(0)
    logits_relay(1)
    gathered_own(1)
    logits_part(1, c, 2)
    gathered_other(1)
    logits_part(1, oc, 3)
    softmax_part(0, c, 0)
    softmax_part(0, oc, 1)
    logits_relay(2)
    logits_relay(3)
    softmax_part(1, c, 2)
    softmax_part(1, oc, 3)

    def merged(parts):
        peak = functools.reduce(jnp.maximum, [p[0:1] for p in parts])
        total = functools.reduce(jnp.add, [p[1:2] * jnp.exp(p[0:1] - peak) for p in parts])
        hit = functools.reduce(jnp.add, [p[2:3] for p in parts])
        return peak, total, hit

    def put(ref, values):
        for i, value in enumerate(values):
            ref[i : i + 1, :] = value

    send(st_send.at[0], st_core, sc_s, sc_r, core_peer)
    got(st_core, sc_r)
    put(st_send.at[1], merged([st_send[0], st_core[...]]))
    st_y[y] = st_send[1]
    for d in range(1, NY):
        send(st_send.at[1], st_y.at[y], sy_s.at[d - 1], sy_r.at[d - 1], y_peer(d))
    for d in range(1, NY):
        got(st_core, sy_r.at[d - 1])
    put(st_send.at[2], merged([st_y[i] for i in range(NY)]))
    st_z[z] = st_send[2]
    for d in range(1, NZ):
        send(st_send.at[2], st_z.at[z], sz_s.at[d - 1], sz_r.at[d - 1], z_peer(d))
    for d in range(1, NZ):
        got(st_core, sz_r.at[d - 1])
    peak, total, hit = merged([st_z[i] for i in range(NZ)])
    lse = peak + jnp.log(total)
    loss[...] = jnp.sum(lse - hit, axis=1, keepdims=True) * (1.0 / 128.0)
    weight = 4.0 * (jnp.full((1, LANES), scale[0], jnp.int32).astype(F32) + 1.0)
    st_x[x, 0:1, :] = weight * jnp.exp(st_send[0, 0:1, :] - lse)
    st_x[x, 1:2, :] = weight * (jnp.exp(hit - lse) - 1.0)
    for d in range(1, NX):
        send(st_x.at[x], st_x.at[x], sx_s.at[d - 1], sx_r.at[d - 1], x_peer(d))
    for k in range(4):
        for d in range(1, NX):
            got(u.at[0, 0, 0], ux_r.at[k, d - 1])
    for d in range(1, NX):
        got(st_core, sx_r.at[d - 1])

    def gradient(l, cc):
        for s in range(NX):
            factor = as_column(st_x[s, 0:1, :], l, cc)
            entry = as_column(st_x[s, 1:2, :], l, cc)
            target = as_column(st_x[s, 2:3, :], l, cc).astype(jnp.int32)
            value = jnp.where(columns == target, entry, u[l, cc, s].astype(F32) * factor)
            grad[l, cc, s * GROUP : (s + 1) * GROUP, :] = value.astype(BF16)

    def hidden_part(l, cc, out, kind):
        def tile(n, _):
            rows = pl.ds(pl.multiple_of(n * 256, 256), 256)
            value = lax.dot_general(
                grad[l, cc], w[rows, :], (((1,), (1,)), ((), ())), preferred_element_type=F32
            )
            out[l, :, rows] = value.astype(kind)
            return 0

        lax.fori_loop(0, FEAT // 256, tile, 0)

    for l in range(2):
        gradient(l, oc)
        hidden_part(l, oc, core_out, BF16)
        send(core_out.at[l], core_in.at[l], gc_s.at[l], gc_r.at[l], core_peer)
        gradient(l, c)
        hidden_part(l, c, keep, F32)

    for l in range(2):
        got(core_in.at[l], gc_r.at[l])
        keep[l] = keep[l] + core_in[l].astype(F32)
        for d in range(1, NY):
            py = (y + d) % NY
            for s in range(NX):
                rows = pl.ds(pl.multiple_of(s * GROUP + py * NZ, NZ), NZ)
                zf[pl.ds(s * NZ, NZ), :] = keep[l, rows, :]
            y_out[l, d - 1] = zf[...].astype(BF16)
            send(y_out.at[l, d - 1], y_in.at[l, d - 1], gy_s.at[l, d - 1], gy_r.at[l, d - 1], y_peer(d))

    def head_tile(n, _):
        rows = pl.ds(pl.multiple_of(n * 256, 256), 256)
        out = jnp.zeros((256, WIDTH), F32)
        for l in range(2):
            for cc in range(2):
                out = out + lax.dot_general(
                    h[l, cc, :, rows], grad[l, cc], (((0,), (0,)), ((), ())), preferred_element_type=F32
                )
        head[rows, :] = out.astype(BF16)
        return 0

    lax.fori_loop(0, FEAT // 256, head_tile, 0)
    head_copy = pltpu.make_async_copy(head, head_hbm, head_sem)
    head_copy.start()

    for l in range(2):
        for d in range(1, NY):
            got(y_in.at[l, d - 1], gy_r.at[l, d - 1])
        for s in range(NX):
            rows = pl.ds(pl.multiple_of(s * GROUP + y * NZ, NZ), NZ)
            zf[pl.ds(s * NZ, NZ), :] = keep[l, rows, :]
        acc = zf[...]
        for d in range(1, NY):
            acc = acc + y_in[l, d - 1].astype(F32)
        for j in range(SUB):
            f[pl.ds(j, NX * NZ, stride=SUB), :] = acc[:, j * LANES : (j + 1) * LANES]
        z_out[l] = f[: NX * NZ * SUB, :].reshape(NX, NZ, SUB, LANES).astype(BF16)
        z_in[l, z] = z_out[l, :, z]
        for d in range(1, NZ):
            send(z_out.at[l, :, (z + d) % NZ], z_in.at[l, z], gz_s.at[l, d - 1], gz_r.at[l, d - 1], z_peer(d))
    for l in range(2):
        for d in range(1, NZ):
            got(z_in.at[l, 0], gz_r.at[l, d - 1])
        acc = z_in[l, 0].astype(F32)
        for i in range(1, NZ):
            acc = acc + z_in[l, i].astype(F32)
        x_out[:, l] = acc.astype(BF16)
    x_in[x] = x_out[x]
    for d in range(1, NX):
        send(x_out.at[(x + d) % NX], x_in.at[x], gx_s.at[d - 1], gx_r.at[d - 1], x_peer(d))
    for d in range(1, NX):
        got(x_in.at[0], gx_r.at[d - 1])
    hs32[...] = x_in[...].astype(F32)
    for xx in range(NX):
        for k in range(SUB):
            at0 = xx * FEAT + k * LANES
            ghid[0, :, at0 : at0 + LANES] = hs32[xx, :, k, :].astype(BF16)
    for copy in sent:
        copy.wait_send()
    head_copy.wait()


def on_device(hidden, out_head, targets, scale_index):
    vmem = pltpu.VMEM
    dma = pltpu.SemaphoreType.DMA
    scratch = [
        vmem((FEAT, WIDTH), BF16),
        vmem((FEAT, WIDTH), BF16),
        vmem((NX, 2, SUB, LANES), F32),
        vmem((NX, 2, SUB, LANES), BF16),
        vmem((2, 2, NX, NY, NZ, SUB, LANES), BF16),
        vmem((CHUNK * SUB, LANES), F32),
        vmem((2, 2, CHUNK, FEAT), BF16),
        vmem((4, NX, GROUP, WIDTH), F32),
        vmem((4, 2, GROUP, HALF), F32),
        vmem((4, 2, GROUP, WIDTH), F32),
        vmem((2, 2, NX, GROUP, WIDTH), BF16),
        vmem((2, 2, CHUNK, WIDTH), BF16),
        vmem((3, 8, LANES), F32),
        vmem((8, LANES), F32),
        vmem((NY, 8, LANES), F32),
        vmem((NZ, 8, LANES), F32),
        vmem((NX, 8, LANES), F32),
        vmem((2, CHUNK, FEAT), BF16),
        vmem((2, CHUNK, FEAT), BF16),
        vmem((2, CHUNK, FEAT), F32),
        vmem((2, NY - 1, NX * NZ, FEAT), BF16),
        vmem((2, NY - 1, NX * NZ, FEAT), BF16),
        vmem((NX * NZ, FEAT), F32),
        vmem((2, NX, NZ, SUB, LANES), BF16),
        vmem((2, NZ, NX, SUB, LANES), BF16),
        vmem((NX, 2, SUB, LANES), BF16),
        vmem((NX, 2, SUB, LANES), BF16),
        dma, dma,
        dma((3,)), dma((3,)), dma((2, 7)), dma((2, 7)),
        dma((2, 3)), dma((2, 3)), dma((2, 4)), dma((2, 4)),
        dma((4, 2)), dma((4, 2)), dma((4, 2)), dma((4, 2)), dma((4, 3)), dma((4, 3)),
        dma, dma, dma((3,)), dma((3,)), dma((7,)), dma((7,)), dma((3,)), dma((3,)),
        dma((2,)), dma((2,)), dma((2, 3)), dma((2, 3)),
        dma((2, 7)), dma((2, 7)), dma((3,)), dma((3,)),
    ]
    in_vmem = pl.BlockSpec(memory_space=pltpu.VMEM)
    head, ghid, loss = pl.pallas_call(
        kernel,
        out_shape=(
            jax.ShapeDtypeStruct((FEAT, WIDTH), BF16),
            jax.ShapeDtypeStruct(hidden.shape, BF16),
            jax.ShapeDtypeStruct((1, 1), F32),
        ),
        in_specs=[
            in_vmem,
            pl.BlockSpec(memory_space=pl.ANY),
            in_vmem,
            pl.BlockSpec(memory_space=pltpu.SMEM),
        ],
        out_specs=(pl.BlockSpec(memory_space=pl.ANY), in_vmem, in_vmem),
        scratch_shapes=scratch,
        compiler_params=pltpu.CompilerParams(
            collective_id=0, has_side_effects=True, vmem_limit_bytes=56 * 2**20
        ),
    )(hidden, out_head, targets, scale_index)
    return head, ghid, loss.reshape(1)


def solution(mesh):
    in_specs = (
        P("section", "vocab", None),
        P("section", "vocab"),
        P("section", None),
        P("section"),
    )
    out_specs = (P("section", "vocab"), P("section", "vocab", None), P("section"))
    return jax.shard_map(
        on_device, mesh=mesh, in_specs=in_specs, out_specs=out_specs, check_vma=False
    )
```

time: 969 us -> 110 us (0.11)
  blocking collectives: 660 us -> 0 us
  waiting for transfers between devices: 162 us -> 0 us
  Pallas kernels: 0 us -> 102 us
  other arithmetic: 50.2 us -> 0 us
  local copies, waits for them, and re-layouts: 50.1 us -> 5.26 us
  matrix products: 20.6 us -> 0 us
  between operations: 16.9 us -> 2.98 us
    unnamed x1 -> x0, blocking collectives: 399 us -> none
    pmax x1 -> x0, blocking collectives: 129 us -> none  [on_device(): peak = lax.pmax(local_peak, 'vocab')]
    psum x1 -> x0, blocking collectives: 124 us -> none  [on_device(): total, target_logit = lax.psum((local_total, local_target), 'vocab')]
    pallas_call x0 -> x1, Pallas kernels: none -> 102 us  [on_device(): pl.pallas_call(kernel, out_shape=(jax.ShapeDtypeStruct((FEAT, WIDTH), BF1...]
    all_gather x2 -> x0, waiting for transfers between devices: 101 us -> none  [the longest x1 79.2 us: on_device(): gathered = lax.all_gather(pieces, 'vocab', axis=1, tiled=True)]
    unnamed x1 -> x0, other arithmetic: 45.2 us -> none
    all_to_all x1 -> x0, waiting for transfers between devices: 33.3 us -> none  [on_device(): lax.all_to_all(grad_part, 'section', split_axis=0, concat_axis=2, tiled=T...]
    reduce_scatter x1 -> x0, waiting for transfers between devices: 28.1 us -> none  [on_device(): lax.psum_scatter(partial_value, 'section', scatter_dimension=0, tiled=True)]
  transfers between devices with their start and end apart: 4 -> 0, of which waited for: 4 -> 0; matrix products, arithmetic and copies ran while one was open for 1% -> 0% of each run, Pallas kernels for 0% -> 0%
where the time goes in v1:
time: 110 us
  Pallas kernels  102 us (93%)
  local copies, waits for them, and re-layouts  5.26 us (5%)
  between operations  2.98 us (3%)
    pallas_call x1, Pallas kernels, on_device(): pl.pallas_call(kernel, out_shape=(jax.ShapeDtypeStruct((FEAT, WIDTH), BF1...  102 us
    unnamed x4, local copies, waits for them, and re-layouts  5.26 us

profile of v1, /device:TPU:2, one launch (start us, length us, event | category | flops | bytes accessed | tf_op | source)
XLA Modules:
  0.0 110.1 jit_solution(1650852636715438528)
XLA Ops:
  1.3 101.9 %shard_map.67 = (bf16[2048,1024]{1,0:T(8,128)(2,1)}, bf16[1,2,8192]{2,1,0:T(2,128)(2,1)}, f32[1,1]{1,0:T(1,128)}) custom-call(bf16[1,2,8192]{2,1,0:T(2,128)(2,1)} %hid.1, bf16[2048,1024]{1,0:T(8,128)(2,1)} %w_hbm.1, s32[1,128]{1,0:T(1,128)} %tgt.1, s32[1]{0:T(128)S(6)} %copy.10.scale), custom_call_target="tpu_custom_call" | custom-call | tf_op jit(solution)/shard_map/pallas_call | solution.py:369
  103.1 0.0 copy-start
  103.1 4.6 %copy.11 = bf16[2048,1024]{1,0:T(8,128)(2,1)} copy(bf16[2048,1024]{1,0:T(8,128)(2,1)} %get-tuple-element.12) | data formatting | bytes 8388608
  107.8 0.0 copy-done
  107.8 0.6 copy.12
Async XLA Ops:
  103.1 4.7 %copy-start = (bf16[1,2,8192]{2,1,0:T(2,128)(2,1)S(1)}, bf16[1,2,8192]{2,1,0:T(2,128)(2,1)}, u32[]{:S(2)}) copy-start(bf16[1,2,8192]{2,1,0:T(2,128)(2,1)} %get-tuple-element.13) | copy-start | bytes 98308

commit v2 on v1

v2 whole, which is shorter than its diff:
```python
import functools

import jax
import jax.numpy as jnp
from jax import lax
from jax.experimental import pallas as pl
from jax.experimental.pallas import tpu as pltpu
from jax.sharding import PartitionSpec as P

MESH = pl.DeviceIdType.MESH
F32 = jnp.float32
BF16 = jnp.bfloat16

NX, NZ, NY = 4, 8, 4
LANES = 128
SUB = 16
FEAT = SUB * LANES
WIDTH = 1024
HALF = WIDTH // 2
GROUP = NY * NZ
CHUNK = NX * GROUP
VMEM_MIB = 46


def kernel(
    hid, w_hbm, tgt, scale, head, ghid, loss,
    w, wt, hs32, hs, g, f, h, part, relay, final, u, grad, hot, hot_w, raw,
    tx, st_send, st_core, st_y, st_z, st_x,
    core_out, core_in, keep, y_out, y_in, zf, z_out, z_in, x_out, x_in,
    w_sem, hx_r, tx_r, hz_r, hy_r, hc_r, rl_r, fn_r, ux_r,
    sc_r, sy_r, sz_r, sx_r, gc_r, gy_r, gz_r, gx_r,
    hx_s, tx_s, hz_s, hy_s, hc_s, rl_s, fn_s, ux_s,
    sc_s, sy_s, sz_s, sx_s, gc_s, gy_s, gz_s, gx_s,
):
    x = lax.axis_index("section")
    v = lax.axis_index("vocab")
    z, y, c = v // 8, (v // 2) % 4, v % 2
    oc = 1 - c

    def at(px, pz, py, pc):
        return (px, (pz * NY + py) * 2 + pc)

    def x_peer(d):
        return at((x + d) % NX, z, y, c)

    def y_peer(d):
        return at(x, z, (y + d) % NY, c)

    def z_peer(d):
        return at(x, (z + d) % NZ, y, c)

    core_peer = at(x, z, y, oc)

    def send(src, dst, s_sem, r_sem, peer):
        pltpu.make_async_remote_copy(
            src_ref=src, dst_ref=dst, send_sem=s_sem, recv_sem=r_sem,
            device_id=peer, device_id_type=MESH,
        ).start()

    def got(ref, sem):
        pltpu.make_async_copy(ref, ref, sem).wait()

    barrier = pltpu.get_barrier_semaphore()
    peers = (
        [x_peer(d) for d in range(1, NX)]
        + [core_peer]
        + [y_peer(d) for d in range(1, NY)]
        + [z_peer(d) for d in range(1, NZ)]
    )
    for peer in peers:
        pl.semaphore_signal(barrier, inc=1, device_id=peer, device_id_type=MESH)

    w_copy = pltpu.make_async_copy(w_hbm, w, w_sem)
    w_copy.start()

    own = hid[0].astype(F32)
    for xx in range(NX):
        for k in range(SUB):
            at0 = xx * FEAT + k * LANES
            hs32[xx, :, k, :] = own[:, at0 : at0 + LANES]
    hs[...] = hs32[...].astype(BF16)

    place = lax.broadcasted_iota(jnp.int32, (128, 128), 0)
    row = lax.broadcasted_iota(jnp.int32, (128, 128), 1)
    pl_l, pl_c, pl_y, pl_z = place // 64, (place // 32) % 2, (place // 8) % 4, place % 8
    match = row == pl_z * 16 + pl_y * 4 + pl_c * 2 + pl_l
    tcol_all = jnp.sum(
        jnp.where(match, tgt[...].astype(F32), 0.0), axis=1, keepdims=True
    )
    tx[x] = jnp.broadcast_to(
        jnp.sum(jnp.where(place == row, tcol_all, 0.0), axis=0, keepdims=True), (8, LANES)
    )
    st_send[...] = jnp.zeros_like(st_send)
    st_x[...] = jnp.zeros_like(st_x)

    pl.semaphore_wait(barrier, len(peers))

    for d in range(1, NX):
        send(hs.at[(x + d) % NX], g.at[:, c, x, y, z], hx_s, hx_r, x_peer(d))
    for d in range(1, NX):
        send(tx.at[x], tx.at[x], tx_s, tx_r, x_peer(d))
    for l in range(2):
        g[l, c, x, y, z] = hs[x, l]
    got(hs.at[pl.ds(0, 3)], hx_r)

    for l in range(2):
        for d in range(1, NZ):
            piece = g.at[l, c, :, y, z]
            send(piece, piece, hz_s, hz_r.at[l], z_peer(d))

    columns = v * WIDTH + lax.broadcasted_iota(jnp.int32, (GROUP, WIDTH), 1)
    lane = lax.broadcasted_iota(jnp.int32, (GROUP, LANES), 1)
    sub = lax.broadcasted_iota(jnp.int32, (GROUP, LANES), 0)

    def spot(l, cc):
        return lane == sub + (l * 2 + cc) * GROUP

    def as_column(line, l, cc):
        return jnp.sum(jnp.where(spot(l, cc), line, 0.0), axis=1, keepdims=True)

    def target_column(s, l, cc):
        return as_column(tx[s, 0:1, :], l, cc).astype(jnp.int32)

    def rows_of(l, cc):
        return pl.ds(pl.multiple_of((l * 2 + cc) * CHUNK, CHUNK), CHUNK)

    got(tx.at[pl.ds(0, 3)], tx_r)
    w_copy.wait()

    def turn(n, _):
        rows = pl.ds(pl.multiple_of(n * 512, 512), 512)
        wt[:, rows] = w[rows, :].T
        return 0

    lax.fori_loop(0, FEAT // 512, turn, 0)

    def target_rows(l, cc):
        for s in range(NX):
            here = columns == target_column(s, l, cc)
            hot[s * GROUP : (s + 1) * GROUP, :] = jnp.where(here, 1.0, 0.0).astype(BF16)
        hot_w[l, cc] = jnp.dot(hot[...], wt[...], preferred_element_type=F32).astype(BF16)

    target_rows(0, c)

    def gathered_z(l):
        got(g.at[l, c, :, 0, pl.ds(0, NZ - 1)], hz_r.at[l])
        block = g.at[l, c, :, y]
        for d in (1, 3, 2):
            send(block, block, hy_s, hy_r.at[l, d - 1], y_peer(d))
        send(block, block, hc_s, hc_r.at[l], core_peer)

    def gathered_own(l):
        for d in (1, 3, 2):
            block = g.at[l, c, :, (y + NY - d) % NY]
            got(block, hy_r.at[l, d - 1])
            send(block, block, hc_s, hc_r.at[l], core_peer)

    def gathered_other(l):
        got(g.at[l, oc], hc_r.at[l])

    def logits_part(l, cc, k):
        f[...] = g[l, cc].reshape(CHUNK * SUB, LANES).astype(F32)
        for j in range(SUB):
            h[rows_of(l, cc), j * LANES : (j + 1) * LANES] = f[pl.ds(j, CHUNK, stride=SUB), :].astype(BF16)
        out = jnp.dot(h[rows_of(l, cc), :], w[...], preferred_element_type=F32)
        part[k] = out.reshape(NX, GROUP, WIDTH)
        far = part.at[k, (x + 2) % NX]
        send(far.at[:, pl.ds(0, HALF)], relay.at[k, 0], rl_s, rl_r.at[k, 0], x_peer(1))
        send(far.at[:, pl.ds(HALF, HALF)], relay.at[k, 1], rl_s, rl_r.at[k, 1], x_peer(3))

    def logits_relay(k):
        right, left = (x + 1) % NX, (x + 3) % NX
        got(relay.at[k, 0], rl_r.at[k, 0])
        part[k, right, :, :HALF] = part[k, right, :, :HALF] + relay[k, 0]
        send(part.at[k, right], final.at[k, 0], fn_s, fn_r.at[k, 0], x_peer(1))
        got(relay.at[k, 1], rl_r.at[k, 1])
        part[k, left, :, HALF:] = part[k, left, :, HALF:] + relay[k, 1]
        send(part.at[k, left], final.at[k, 1], fn_s, fn_r.at[k, 1], x_peer(3))

    def softmax_part(l, cc, k):
        got(final.at[k, 0], fn_r.at[k, 0])
        got(final.at[k, 1], fn_r.at[k, 1])
        logits = part[k, x] + final[k, 0] + final[k, 1]
        peak = jnp.max(logits, axis=1, keepdims=True)
        raised = jnp.exp(logits - peak)
        total = jnp.sum(raised, axis=1, keepdims=True)
        here = columns == target_column(x, l, cc)
        hit = jnp.sum(jnp.where(here, logits, 0.0), axis=1, keepdims=True)
        u[l, cc, x] = jnp.where(here, 0.0, raised).astype(BF16)
        for i, value in enumerate((peak, total, hit)):
            line = jnp.sum(jnp.where(spot(l, cc), value, 0.0), axis=0, keepdims=True)
            st_send[l, 0, i : i + 1, :] = st_send[l, 0, i : i + 1, :] + line

    def raised_out(l, cc, k):
        for d in (1, 3, 2):
            send(u.at[l, cc, x], u.at[l, cc, x], ux_s, ux_r.at[k], x_peer(d))

    def merged(parts):
        peak = functools.reduce(jnp.maximum, [p[0:1] for p in parts])
        total = functools.reduce(jnp.add, [p[1:2] * jnp.exp(p[0:1] - peak) for p in parts])
        hit = functools.reduce(jnp.add, [p[2:3] for p in parts])
        return peak, total, hit

    def put(ref, values):
        for i, value in enumerate(values):
            ref[i : i + 1, :] = value

    def stats_core(l):
        send(st_send.at[l, 0], st_core.at[l], sc_s, sc_r.at[l], core_peer)

    def stats_y(l):
        got(st_core.at[l], sc_r.at[l])
        put(st_send.at[l, 1], merged([st_send[l, 0], st_core[l]]))
        st_y[l, y] = st_send[l, 1]
        for d in range(1, NY):
            send(st_send.at[l, 1], st_y.at[l, y], sy_s, sy_r.at[l], y_peer(d))

    def stats_z(l):
        got(st_y.at[l, pl.ds(0, NY - 1)], sy_r.at[l])
        put(st_send.at[l, 2], merged([st_y[l, i] for i in range(NY)]))
        st_z[l, z] = st_send[l, 2]
        for d in range(1, NZ):
            send(st_send.at[l, 2], st_z.at[l, z], sz_s, sz_r.at[l], z_peer(d))

    weight = 4.0 * (jnp.full((1, LANES), scale[0], jnp.int32).astype(F32) + 1.0)

    def stats_x(l):
        got(st_z.at[l, pl.ds(0, NZ - 1)], sz_r.at[l])
        peak, total, hit = merged([st_z[l, i] for i in range(NZ)])
        mine = lax.broadcasted_iota(jnp.int32, (1, LANES), 1) // 64 == l
        lse = peak + jnp.log(jnp.where(mine, total, 1.0))
        st_x[l, x, 0:1, :] = weight * jnp.exp(st_send[l, 0, 0:1, :] - lse)
        st_x[l, x, 1:2, :] = weight * (jnp.exp(hit - lse) - 1.0)
        for d in range(1, NX):
            send(st_x.at[l, x], st_x.at[l, x], sx_s, sx_r.at[l], x_peer(d))
        return jnp.sum(jnp.where(mine, lse - hit, 0.0), axis=1, keepdims=True)

    def product(l, cc, k):
        got(u.at[l, cc, pl.ds(0, 3)], ux_r.at[k])
        value = u[l, cc].reshape(CHUNK, WIDTH)
        raw[l, cc] = jnp.dot(value, wt[...], preferred_element_type=F32).reshape(NX, GROUP, FEAT)

    def scaled(l, cc, s):
        factor = as_column(st_x[l, s, 0:1, :], l, cc)
        entry = as_column(st_x[l, s, 1:2, :], l, cc)
        rows = pl.ds(s * GROUP, GROUP)
        return factor * raw[l, cc, s] + entry * hot_w[l, cc, rows, :].astype(F32)

    def hidden_core(l):
        got(st_x.at[l, pl.ds(0, NX - 1)], sx_r.at[l])
        for s in range(NX):
            core_out[l, s * GROUP : (s + 1) * GROUP, :] = scaled(l, oc, s).astype(BF16)
        send(core_out.at[l], core_in.at[l], gc_s, gc_r.at[l], core_peer)
        for s in range(NX):
            keep[l, s * GROUP : (s + 1) * GROUP, :] = scaled(l, c, s)

    def slab(l, py):
        for s in range(NX):
            rows = pl.ds(pl.multiple_of(s * GROUP + py * NZ, NZ), NZ)
            zf[pl.ds(s * NZ, NZ), :] = keep[l, rows, :]
        return zf[...]

    def hidden_y(l):
        got(core_in.at[l], gc_r.at[l])
        keep[l] = keep[l] + core_in[l].astype(F32)
        for d in (1, 3, 2):
            y_out[l, d - 1] = slab(l, (y + d) % NY).astype(BF16)
            send(y_out.at[l, d - 1], y_in.at[l, d - 1], gy_s, gy_r.at[l], y_peer(d))

    def hidden_z(l):
        got(y_in.at[l], gy_r.at[l])
        acc = slab(l, y)
        for d in range(1, NY):
            acc = acc + y_in[l, d - 1].astype(F32)
        for j in range(SUB):
            f[pl.ds(j, NX * NZ, stride=SUB), :] = acc[:, j * LANES : (j + 1) * LANES]
        z_out[l] = f[: NX * NZ * SUB, :].reshape(NX, NZ, SUB, LANES).astype(BF16)
        z_in[l, z] = z_out[l, :, z]
        for d in range(1, NZ):
            send(z_out.at[l, :, (z + d) % NZ], z_in.at[l, z], gz_s, gz_r.at[l], z_peer(d))

    def hidden_x(l):
        got(z_in.at[l, pl.ds(0, NZ - 1)], gz_r.at[l])
        acc = z_in[l, 0].astype(F32)
        for i in range(1, NZ):
            acc = acc + z_in[l, i].astype(F32)
        x_out[:, l] = acc.astype(BF16)

    def gradient(l, cc):
        for s in range(NX):
            factor = as_column(st_x[l, s, 0:1, :], l, cc)
            entry = as_column(st_x[l, s, 1:2, :], l, cc)
            here = columns == target_column(s, l, cc)
            value = jnp.where(here, entry, u[l, cc, s].astype(F32) * factor)
            at0 = pl.multiple_of((l * 2 + cc) * CHUNK + s * GROUP, GROUP)
            grad[pl.ds(at0, GROUP), :] = value.astype(BF16)

    gathered_z(0)
    target_rows(0, oc)
    gathered_z(1)
    target_rows(1, c)
    gathered_own(0)
    logits_part(0, c, 0)
    gathered_other(0)
    logits_part(0, oc, 1)
    target_rows(1, oc)
    logits_relay(0)
    logits_relay(1)
    gathered_own(1)
    logits_part(1, c, 2)
    gathered_other(1)
    logits_part(1, oc, 3)
    softmax_part(0, c, 0)
    softmax_part(0, oc, 1)
    stats_core(0)
    logits_relay(2)
    stats_y(0)
    logits_relay(3)
    raised_out(0, c, 0)
    raised_out(0, oc, 1)
    stats_z(0)
    softmax_part(1, c, 2)
    loss0 = stats_x(0)
    softmax_part(1, oc, 3)
    stats_core(1)
    raised_out(1, c, 2)
    raised_out(1, oc, 3)
    product(0, oc, 1)
    stats_y(1)
    product(0, c, 0)
    hidden_core(0)
    stats_z(1)
    hidden_y(0)
    product(1, oc, 3)
    product(1, c, 2)
    loss1 = stats_x(1)
    loss[...] = (loss0 + loss1) * (1.0 / 128.0)
    gradient(0, 0)
    gradient(0, 1)
    hidden_z(0)
    hidden_core(1)
    hidden_y(1)
    gradient(1, 0)
    gradient(1, 1)

    def head_tile(n, _):
        rows = pl.ds(pl.multiple_of(n * 512, 512), 512)
        out = lax.dot_general(
            h[:, rows], grad[...], (((0,), (0,)), ((), ())), preferred_element_type=F32
        )
        head[rows, :] = out.astype(BF16)
        return 0

    lax.fori_loop(0, FEAT // 512, head_tile, 0)
    hidden_x(0)
    hidden_z(1)
    hidden_x(1)
    x_in[x] = x_out[x]
    for d in range(1, NX):
        send(x_out.at[(x + d) % NX], x_in.at[x], gx_s, gx_r, x_peer(d))
    got(x_in.at[pl.ds(0, NX - 1)], gx_r)
    hs32[...] = x_in[...].astype(F32)
    for xx in range(NX):
        for k in range(SUB):
            at0 = xx * FEAT + k * LANES
            ghid[0, :, at0 : at0 + LANES] = hs32[xx, :, k, :].astype(BF16)

    got(hs.at[pl.ds(0, 3)], hx_s)
    got(tx.at[pl.ds(0, 3)], tx_s)
    got(g.at[:, 0, :, 0, pl.ds(0, NZ - 1)], hz_s)
    got(g.at[:, 0, :, pl.ds(0, NY - 1)], hy_s)
    got(g.at[:, 0], hc_s)
    got(relay, rl_s)
    got(final, fn_s)
    got(u.at[:, :, pl.ds(0, 3)], ux_s)
    got(st_core, sc_s)
    got(st_y.at[:, pl.ds(0, NY - 1)], sy_s)
    got(st_z.at[:, pl.ds(0, NZ - 1)], sz_s)
    got(st_x.at[:, pl.ds(0, NX - 1)], sx_s)
    got(core_in, gc_s)
    got(y_in, gy_s)
    got(z_in.at[:, pl.ds(0, NZ - 1)], gz_s)
    got(x_in.at[pl.ds(0, NX - 1)], gx_s)


def on_device(hidden, out_head, targets, scale_index):
    vmem = pltpu.VMEM
    dma = pltpu.SemaphoreType.DMA
    scratch = [
        vmem((FEAT, WIDTH), BF16),
        vmem((WIDTH, FEAT), BF16),
        vmem((NX, 2, SUB, LANES), F32),
        vmem((NX, 2, SUB, LANES), BF16),
        vmem((2, 2, NX, NY, NZ, SUB, LANES), BF16),
        vmem((CHUNK * SUB, LANES), F32),
        vmem((4 * CHUNK, FEAT), BF16),
        vmem((4, NX, GROUP, WIDTH), F32),
        vmem((4, 2, GROUP, HALF), F32),
        vmem((4, 2, GROUP, WIDTH), F32),
        vmem((2, 2, NX, GROUP, WIDTH), BF16),
        vmem((4 * CHUNK, WIDTH), BF16),
        vmem((CHUNK, WIDTH), BF16),
        vmem((2, 2, CHUNK, FEAT), BF16),
        vmem((2, 2, NX, GROUP, FEAT), F32),
        vmem((NX, 8, LANES), F32),
        vmem((2, 3, 8, LANES), F32),
        vmem((2, 8, LANES), F32),
        vmem((2, NY, 8, LANES), F32),
        vmem((2, NZ, 8, LANES), F32),
        vmem((2, NX, 8, LANES), F32),
        vmem((2, CHUNK, FEAT), BF16),
        vmem((2, CHUNK, FEAT), BF16),
        vmem((2, CHUNK, FEAT), F32),
        vmem((2, NY - 1, NX * NZ, FEAT), BF16),
        vmem((2, NY - 1, NX * NZ, FEAT), BF16),
        vmem((NX * NZ, FEAT), F32),
        vmem((2, NX, NZ, SUB, LANES), BF16),
        vmem((2, NZ, NX, SUB, LANES), BF16),
        vmem((NX, 2, SUB, LANES), BF16),
        vmem((NX, 2, SUB, LANES), BF16),
        dma, dma, dma, dma((2,)), dma((2, 3)), dma((2,)), dma((4, 2)), dma((4, 2)), dma((4,)),
        dma((2,)), dma((2,)), dma((2,)), dma((2,)), dma((2,)), dma((2,)), dma((2,)), dma,
    ] + [dma] * 16
    in_vmem = pl.BlockSpec(memory_space=pltpu.VMEM)
    head, ghid, loss = pl.pallas_call(
        kernel,
        out_shape=(
            jax.ShapeDtypeStruct((FEAT, WIDTH), BF16),
            jax.ShapeDtypeStruct(hidden.shape, BF16),
            jax.ShapeDtypeStruct((1, 1), F32),
        ),
        in_specs=[
            in_vmem,
            pl.BlockSpec(memory_space=pl.ANY),
            in_vmem,
            pl.BlockSpec(memory_space=pltpu.SMEM),
        ],
        out_specs=(in_vmem, in_vmem, in_vmem),
        scratch_shapes=scratch,
        compiler_params=pltpu.CompilerParams(
            collective_id=0, has_side_effects=True, vmem_limit_bytes=VMEM_MIB * 2**20
        ),
    )(hidden, out_head, targets, scale_index)
    return head, ghid, loss.reshape(1)


def solution(mesh):
    in_specs = (
        P("section", "vocab", None),
        P("section", "vocab"),
        P("section", None),
        P("section"),
    )
    out_specs = (P("section", "vocab"), P("section", "vocab", None), P("section"))
    return jax.shard_map(
        on_device, mesh=mesh, in_specs=in_specs, out_specs=out_specs, check_vma=False
    )
```

time: 110 us -> 97.4 us (0.89)
  Pallas kernels: 102 us -> 89.9 us
  local copies, waits for them, and re-layouts: 5.26 us -> 4.04 us
    pallas_call x1, Pallas kernels: 102 us -> 89.9 us  [on_device(): pl.pallas_call(kernel, out_shape=(jax.ShapeDtypeStruct((FEAT, WIDTH), BF1...]
    unnamed x4 -> x6, local copies, waits for them, and re-layouts: 5.26 us -> 4.04 us
where the time goes in v2:
time: 97.4 us; the launch traced here: 97 us
  Pallas kernels  89.9 us (92%)
  local copies, waits for them, and re-layouts  4.04 us (4%)
  between operations  3.06 us (3%)
    pallas_call x1, Pallas kernels, on_device(): pl.pallas_call(kernel, out_shape=(jax.ShapeDtypeStruct((FEAT, WIDTH), BF1...  89.9 us
    unnamed x6, local copies, waits for them, and re-layouts  4.04 us

profile of v2, /device:TPU:2, one launch (start us, length us, event | category | flops | bytes accessed | tf_op | source)
XLA Modules:
  0.0 97.0 jit_solution(12613179660219754290)
XLA Ops:
  1.3 0.0 copy-start
  1.3 0.7 copy-done
  2.0 0.0 copy-start.1
  2.0 0.7 copy-done.1
  2.7 89.9 %shard_map.67 = (bf16[2048,1024]{1,0:T(8,128)(2,1)S(1)}, bf16[1,2,8192]{2,1,0:T(2,128)(2,1)S(1)}, f32[1,1]{1,0:T(1,128)}) custom-call(bf16[1,2,8192]{2,1,0:T(2,128)(2,1)S(1)} %copy-done, bf16[2048,1024]{1,0:T(8,128)(2,1)} %w_hbm.1, s32[1,128]{1,0:T(1,128)S(1)} %copy-done.1, s32[1]{0:T(128)S(6)} %copy.10.scale), custom_call_target="tpu_custom_call" | custom-call | tf_op jit(solution)/shard_map/pallas_call | solution.py:425
  92.6 2.0 %copy.11 = bf16[2048,1024]{1,0:T(8,128)(2,1)} copy(bf16[2048,1024]{1,0:T(8,128)(2,1)S(1)} %get-tuple-element.12) | data formatting | bytes 8388608
  94.6 0.6 copy.12
Async XLA Ops:
  1.3 0.8 copy-start
  2.0 0.7 copy-start.1

commit v3 on v2

v3 whole, which is shorter than its diff:
```python
import functools

import jax
import jax.numpy as jnp
from jax import lax
from jax.experimental import pallas as pl
from jax.experimental.pallas import tpu as pltpu
from jax.sharding import PartitionSpec as P

MESH = pl.DeviceIdType.MESH
F32 = jnp.float32
BF16 = jnp.bfloat16

NX, NZ, NY = 4, 8, 4
LANES = 128
SUB = 16
FEAT = SUB * LANES
WIDTH = 1024
HALF = WIDTH // 2
GROUP = 2 * NZ
CHUNK = NX * GROUP
PART = NY * CHUNK
VMEM_MIB = 46
Z_ORDER = (4, 3, 5, 2, 6, 1, 7)


def kernel(
    hid_hbm, w_hbm, tgt_hbm, scale, head, ghid, loss,
    hid, tgt, w, wt, hs32, hs, g, f, h, part, relay, final, u, grad, hot, hot_w,
    tx, st_raw, st_own, st_core, st_y, st_z, st_end,
    core_out, core_in, both, y_out, y_in, z_out, z_in, x_out, x_in,
    tcore_in, ty_out, ty_in, tz_out, tz_in,
    hid_sem, tgt_sem, w_sem, hx_r, tx_r, hz_r, hy_r, hc_r, rl_r, fn_r, ux_r,
    sc_r, sy_r, sz_r, sx_r, gc_r, gy_r, gz_r, gx_r,
    hx_s, tx_s, hz_s, hy_s, hc_s, rl_s, fn_s, ux_s,
    sc_s, sy_s, sz_s, sx_s, gc_s, gy_s, gz_s, gx_s, tc_r, ty_r, tz_r, tc_s, ty_s, tz_s,
):
    x = lax.axis_index("section")
    v = lax.axis_index("vocab")
    z, y, c = v // 8, (v // 2) % 4, v % 2
    oc = 1 - c

    def at(px, pz, py, pc):
        return (px, (pz * NY + py) * 2 + pc)

    def x_peer(d):
        return at((x + d) % NX, z, y, c)

    def y_peer(d):
        return at(x, z, (y + d) % NY, c)

    def z_peer(d):
        return at(x, (z + d) % NZ, y, c)

    core_peer = at(x, z, y, oc)

    def send(src, dst, s_sem, r_sem, peer):
        pltpu.make_async_remote_copy(
            src_ref=src, dst_ref=dst, send_sem=s_sem, recv_sem=r_sem,
            device_id=peer, device_id_type=MESH,
        ).start()

    def got(ref, sem):
        pltpu.make_async_copy(ref, ref, sem).wait()

    hid_copy = pltpu.make_async_copy(hid_hbm, hid, hid_sem)
    hid_copy.start()
    tgt_copy = pltpu.make_async_copy(tgt_hbm, tgt, tgt_sem)
    tgt_copy.start()
    barrier = pltpu.get_barrier_semaphore()
    peers = (
        [x_peer(d) for d in range(1, NX)]
        + [core_peer]
        + [y_peer(d) for d in range(1, NY)]
        + [z_peer(d) for d in range(1, NZ)]
    )
    for peer in peers:
        pl.semaphore_signal(barrier, inc=1, device_id=peer, device_id_type=MESH)

    w_copy = pltpu.make_async_copy(w_hbm, w, w_sem)
    w_copy.start()

    hid_copy.wait()
    own = hid[0].astype(F32)
    for xx in range(NX):
        for k in range(SUB):
            at0 = xx * FEAT + k * LANES
            hs32[xx, :, k, :] = own[:, at0 : at0 + LANES]
    hs[...] = hs32[...].astype(BF16)

    tgt_copy.wait()
    place = lax.broadcasted_iota(jnp.int32, (128, 128), 0)
    row = lax.broadcasted_iota(jnp.int32, (128, 128), 1)
    pl_l, pl_y, pl_c, pl_z = place // 64, (place // 16) % 4, (place // 8) % 2, place % 8
    match = row == pl_z * 16 + pl_y * 4 + pl_c * 2 + pl_l
    tcol_all = jnp.sum(
        jnp.where(match, tgt[...].astype(F32), 0.0), axis=1, keepdims=True
    )
    weight = 4.0 * (jnp.full((1, LANES), scale[0], jnp.int32).astype(F32) + 1.0)
    tx[x] = jnp.zeros((8, LANES), F32)
    tx[x, 0:1, :] = jnp.sum(jnp.where(place == row, tcol_all, 0.0), axis=0, keepdims=True)
    tx[x, 1:2, :] = weight
    st_raw[...] = jnp.zeros_like(st_raw)
    st_own[...] = jnp.zeros_like(st_own)

    pl.semaphore_wait(barrier, len(peers))

    for d in range(1, NX):
        send(hs.at[(x + d) % NX], g.at[:, y, x, c, z], hx_s, hx_r, x_peer(d))
    for d in range(1, NX):
        send(tx.at[x], tx.at[x], tx_s, tx_r, x_peer(d))
    for l in range(2):
        g[l, y, x, c, z] = hs[x, l]
    got(hs.at[pl.ds(0, 3)], hx_r)

    for l in range(2):
        for d in Z_ORDER:
            piece = g.at[l, y, :, c, z]
            send(piece, piece, hz_s, hz_r.at[l], z_peer(d))

    columns = v * WIDTH + lax.broadcasted_iota(jnp.int32, (GROUP, WIDTH), 1)
    lane = lax.broadcasted_iota(jnp.int32, (GROUP, LANES), 1)
    sub = lax.broadcasted_iota(jnp.int32, (GROUP, LANES), 0)

    def spot(s, py):
        return lane == sub + (s % 2) * 64 + py * GROUP

    def as_column(lines, s, py):
        line = lines[s // 2 : s // 2 + 1]
        return jnp.sum(jnp.where(spot(s, py), line, 0.0), axis=1, keepdims=True)

    def target_column(s, l, py):
        here = lane == sub + (l * NY + py) * GROUP
        return jnp.sum(jnp.where(here, tx[s, 0:1, :], 0.0), axis=1, keepdims=True).astype(jnp.int32)

    def rows_of(l, py, s=0, count=CHUNK):
        return pl.ds(pl.multiple_of((l * NY + py) * CHUNK + s * GROUP, GROUP), count)

    got(tx.at[pl.ds(0, 3)], tx_r)
    w_copy.wait()

    def turn(n, _):
        rows = pl.ds(pl.multiple_of(n * 512, 512), 512)
        wt[:, rows] = w[rows, :].T
        return 0

    lax.fori_loop(0, FEAT // 512, turn, 0)

    for l in range(2):
        for py in range(NY):
            for s in range(NX):
                here = columns == target_column(s, l, py)
                at0 = py * CHUNK + s * GROUP
                hot[at0 : at0 + GROUP, :] = jnp.where(here, 1.0, 0.0).astype(BF16)
        out = jnp.dot(hot[...], wt[...], preferred_element_type=F32)
        for cc in range(2):
            for py in range(NY):
                for s in range(0, NX, 2):
                    at0 = [py * CHUNK + (s + i) * GROUP + cc * NZ for i in range(2)]
                    pair = jnp.concatenate([out[i : i + NZ] for i in at0], axis=0)
                    hot_w[l, cc, py, s * NZ : (s + 2) * NZ, :] = pair.astype(BF16)

    def from_y(d):
        return (y + NY - d) % NY

    def gathered_z(l):
        got(g.at[l, 0, :, 0, pl.ds(0, NZ - 1)], hz_r.at[l])
        block = g.at[l, y, :, c]
        for d in (1, 3, 2):
            send(block, block, hy_s, hy_r.at[l, d - 1], y_peer(d))
        send(block, block, hc_s, hc_r.at[l, 0], core_peer)

    def gathered_y(l, d):
        block = g.at[l, from_y(d), :, c]
        got(block, hy_r.at[l, d - 1])
        send(block, block, hc_s, hc_r.at[l, d], core_peer)

    def logits_part(l, d):
        py, k = from_y(d), l * NY + d
        got(g.at[l, py, :, oc], hc_r.at[l, d])
        f[...] = g[l, py].reshape(CHUNK * SUB, LANES).astype(F32)
        rows = rows_of(l, py)
        for j in range(SUB):
            h[rows, j * LANES : (j + 1) * LANES] = f[pl.ds(j, CHUNK, stride=SUB), :].astype(BF16)
        out = jnp.dot(h[rows, :], w[...], preferred_element_type=F32)
        part[k] = out.reshape(NX, GROUP, WIDTH)
        far = part.at[k, (x + 2) % NX]
        send(far.at[:, pl.ds(0, HALF)], relay.at[k, 0], rl_s, rl_r.at[k, 0], x_peer(1))
        send(far.at[:, pl.ds(HALF, HALF)], relay.at[k, 1], rl_s, rl_r.at[k, 1], x_peer(3))

    def logits_relay(l, d):
        k = l * NY + d
        right, left = (x + 1) % NX, (x + 3) % NX
        got(relay.at[k, 0], rl_r.at[k, 0])
        part[k, right, :, :HALF] = part[k, right, :, :HALF] + relay[k, 0]
        send(part.at[k, right], final.at[k, 0], fn_s, fn_r.at[k, 0], x_peer(1))
        got(relay.at[k, 1], rl_r.at[k, 1])
        part[k, left, :, HALF:] = part[k, left, :, HALF:] + relay[k, 1]
        send(part.at[k, left], final.at[k, 1], fn_s, fn_r.at[k, 1], x_peer(3))

    def softmax_part(l, d):
        py, k = from_y(d), l * NY + d
        got(final.at[k, 0], fn_r.at[k, 0])
        got(final.at[k, 1], fn_r.at[k, 1])
        logits = part[k, x] + final[k, 0] + final[k, 1]
        peak = jnp.max(logits, axis=1, keepdims=True)
        raised = jnp.exp(logits - peak)
        total = jnp.sum(raised, axis=1, keepdims=True)
        here = columns == target_column(x, l, py)
        hit = jnp.sum(jnp.where(here, logits, 0.0), axis=1, keepdims=True)
        u[l, py, x] = jnp.where(here, 0.0, raised).astype(BF16)
        tile = st_raw[l, x]
        which = lax.broadcasted_iota(jnp.int32, (8, LANES), 0)
        for i, value in enumerate((peak, total, hit)):
            line = jnp.sum(jnp.where(spot(x, py), value, 0.0), axis=0, keepdims=True)
            tile = tile + jnp.where(which == 2 * i + x // 2, line, 0.0)
        st_raw[l, x] = tile

    def raised_out(l, d):
        mine = u.at[l, from_y(d), x]
        for other in (1, 3, 2):
            send(mine, mine, ux_s, ux_r.at[l, d], x_peer(other))

    def merged(parts):
        peak = functools.reduce(jnp.maximum, [p[0:2] for p in parts])
        total = functools.reduce(jnp.add, [p[2:4] * jnp.exp(p[0:2] - peak) for p in parts])
        hit = functools.reduce(jnp.add, [p[4:6] for p in parts])
        return peak, total, hit

    def put(ref, values):
        for i, value in enumerate(values):
            ref[2 * i : 2 * i + 2, :] = value

    def stats_x(l):
        for d in range(1, NX):
            send(st_raw.at[l, x], st_raw.at[l, x], sx_s, sx_r.at[l], x_peer(d))

    def stats_core(l):
        got(st_raw.at[l, pl.ds(0, NX - 1)], sx_r.at[l])
        st_own[l, 0] = st_raw[l, 0] + st_raw[l, 1] + st_raw[l, 2] + st_raw[l, 3]
        send(st_own.at[l, 0], st_core.at[l], sc_s, sc_r.at[l], core_peer)

    def stats_y(l):
        got(st_core.at[l], sc_r.at[l])
        put(st_own.at[l, 1], merged([st_own[l, 0], st_core[l]]))
        st_y[l, y] = st_own[l, 1]
        for d in range(1, NY):
            send(st_own.at[l, 1], st_y.at[l, y], sy_s, sy_r.at[l], y_peer(d))

    def stats_z(l):
        got(st_y.at[l, pl.ds(0, NY - 1)], sy_r.at[l])
        put(st_own.at[l, 2], merged([st_y[l, i] for i in range(NY)]))
        st_z[l, z] = st_own[l, 2]
        for d in Z_ORDER:
            send(st_own.at[l, 2], st_z.at[l, z], sz_s, sz_r.at[l], z_peer(d))

    def stats_end(l):
        got(st_z.at[l, pl.ds(0, NZ - 1)], sz_r.at[l])
        peak, total, hit = merged([st_z[l, i] for i in range(NZ)])
        lse = peak + jnp.log(total)
        lower = lax.broadcasted_iota(jnp.int32, (1, LANES), 1) < 64
        lines = [jnp.where(lower, tx[s, 1:2, :], tx[s + 1, 1:2, :]) for s in (0, 2)]
        weights = jnp.concatenate(lines, axis=0)
        st_end[l, 0:2, :] = weights * jnp.exp(st_own[l, 0, 0:2, :] - lse)
        st_end[l, 2:4, :] = weights * (jnp.exp(hit - lse) - 1.0)
        st_end[l, 4:6, :] = lse
        st_end[l, 6:8, :] = weights
        mine = (lax.broadcasted_iota(jnp.int32, (2, LANES), 1) // 64 == x % 2) & (
            lax.broadcasted_iota(jnp.int32, (2, LANES), 0) == x // 2
        )
        gap = jnp.where(mine, lse - hit, 0.0)
        return jnp.sum(gap[0:1] + gap[1:2], axis=1, keepdims=True)

    small = lax.broadcasted_iota(jnp.int32, (NZ, LANES), 1)
    small_sub = lax.broadcasted_iota(jnp.int32, (NZ, LANES), 0)

    def own_column(lines, py):
        parts = []
        for s in range(NX):
            here = small == small_sub + (s % 2) * 64 + py * GROUP + c * NZ
            line = lines[s // 2 : s // 2 + 1]
            parts.append(jnp.sum(jnp.where(here, line, 0.0), axis=1, keepdims=True))
        return jnp.concatenate(parts, axis=0)

    def product(l, d):
        py = from_y(d)
        got(u.at[l, py, pl.ds(0, NX - 1)], ux_r.at[l, d])
        out = jnp.dot(u[l, py].reshape(CHUNK, WIDTH), wt[...], preferred_element_type=F32)
        for s in range(NX):
            for cc in range(2):
                at0 = s * GROUP + cc * NZ
                both[l, cc, py, s * NZ : (s + 1) * NZ, :] = out[at0 : at0 + NZ]
        core_out[l, py] = both[l, oc, py].astype(BF16)
        send(core_out.at[l, py], core_in.at[l, py], gc_s, gc_r.at[l, d], core_peer)

    def chip_sum(l, py):
        peak = st_own[l, 1, 0:2, :]
        mine = own_column(jnp.exp(st_own[l, 0, 0:2, :] - peak), py)
        other = own_column(jnp.exp(st_core[l, 0:2, :] - peak), py)
        return mine * both[l, c, py] + other * core_in[l, py].astype(F32)

    def hidden_y(l, d):
        py = from_y(d)
        got(core_in.at[l, py], gc_r.at[l, d])
        y_out[l, d - 1] = chip_sum(l, py).astype(BF16)
        send(y_out.at[l, d - 1], y_in.at[l, d - 1], gy_s, gy_r.at[l], y_peer(NY - d))

    def as_tiles(acc, out):
        for j in range(SUB):
            f[pl.ds(j, NX * NZ, stride=SUB), :] = acc[:, j * LANES : (j + 1) * LANES]
        out[...] = f[: NX * NZ * SUB, :].reshape(NX, NZ, SUB, LANES).astype(BF16)

    def hidden_z(l):
        got(core_in.at[l, y], gc_r.at[l, 0])
        got(y_in.at[l], gy_r.at[l])
        lse, weights = st_end[l, 4:6, :], st_end[l, 6:8, :]
        acc = own_column(weights * jnp.exp(st_y[l, y, 0:2, :] - lse), y) * chip_sum(l, y)
        for d in range(1, NY):
            factor = own_column(weights * jnp.exp(st_y[l, (y + d) % NY, 0:2, :] - lse), y)
            acc = acc + factor * y_in[l, d - 1].astype(F32)
        as_tiles(acc, z_out.at[l])
        z_in[l, z] = z_out[l, :, z]
        for d in Z_ORDER:
            send(z_out.at[l, :, (z + d) % NZ], z_in.at[l, z], gz_s, gz_r.at[l], z_peer(d))

    def hidden_x(l):
        got(z_in.at[l, pl.ds(0, NZ - 1)], gz_r.at[l])
        acc = z_in[l, 0].astype(F32)
        for i in range(1, NZ):
            acc = acc + z_in[l, i].astype(F32)
        at_target = tz_in[l, 0].astype(F32)
        for i in range(1, NZ):
            at_target = at_target + tz_in[l, i].astype(F32)
        line_at = lax.broadcasted_iota(jnp.int32, (1, LANES), 1)
        for s in range(NX):
            here = line_at == (s % 2) * 64 + y * GROUP + c * NZ + z
            line = st_end[l, 2 + s // 2 : 3 + s // 2, :]
            entry = jnp.sum(jnp.where(here, line, 0.0), axis=1, keepdims=True)
            x_out[s, l] = (acc[s] + entry * at_target[s]).astype(BF16)

    def target_core(l):
        send(hot_w.at[l, oc], tcore_in.at[l], tc_s, tc_r.at[l], core_peer)

    def target_y(l):
        got(tcore_in.at[l], tc_r.at[l])
        for d in (1, 3, 2):
            py = (y + d) % NY
            ty_out[l, d - 1] = (hot_w[l, c, py].astype(F32) + tcore_in[l, py].astype(F32)).astype(BF16)
            send(ty_out.at[l, d - 1], ty_in.at[l, d - 1], ty_s, ty_r.at[l], y_peer(d))

    def target_z(l):
        got(ty_in.at[l], ty_r.at[l])
        acc = hot_w[l, c, y].astype(F32) + tcore_in[l, y].astype(F32)
        for d in range(1, NY):
            acc = acc + ty_in[l, d - 1].astype(F32)
        as_tiles(acc, tz_out.at[l])
        tz_in[l, z] = tz_out[l, :, z]
        for d in Z_ORDER:
            send(tz_out.at[l, :, (z + d) % NZ], tz_in.at[l, z], tz_s, tz_r.at[l], z_peer(d))

    def target_end(l):
        got(tz_in.at[l, pl.ds(0, NZ - 1)], tz_r.at[l])

    def gradient(l):
        for py in range(NY):
            for s in range(NX):
                factor = as_column(st_end[l, 0:2, :], s, py)
                entry = as_column(st_end[l, 2:4, :], s, py)
                here = columns == target_column(s, l, py)
                value = jnp.where(here, entry, u[l, py, s].astype(F32) * factor)
                grad[rows_of(l, py, s, GROUP), :] = value.astype(BF16)

    gathered_z(0)
    logits_part(0, 0)
    gathered_z(1)
    logits_part(1, 0)
    target_core(0)
    gathered_y(0, 1)
    gathered_y(0, 3)
    logits_relay(0, 0)
    logits_part(0, 1)
    logits_relay(1, 0)
    logits_part(0, 3)
    gathered_y(0, 2)
    target_core(1)
    logits_part(0, 2)
    target_y(0)
    softmax_part(0, 0)
    raised_out(0, 0)
    gathered_y(1, 1)
    logits_relay(0, 1)
    gathered_y(1, 3)
    logits_part(1, 1)
    logits_relay(0, 3)
    softmax_part(1, 0)
    logits_part(1, 3)
    logits_relay(0, 2)
    gathered_y(1, 2)
    target_y(1)
    softmax_part(0, 1)
    raised_out(0, 1)
    logits_part(1, 2)
    softmax_part(0, 3)
    raised_out(0, 3)
    logits_relay(1, 1)
    logits_relay(1, 3)
    product(0, 0)
    softmax_part(0, 2)
    stats_x(0)
    logits_relay(1, 2)
    raised_out(0, 2)
    product(0, 1)
    product(0, 3)
    softmax_part(1, 1)
    raised_out(1, 1)
    softmax_part(1, 3)
    raised_out(1, 3)
    stats_core(0)
    softmax_part(1, 2)
    stats_x(1)
    raised_out(1, 2)
    raised_out(1, 0)
    stats_y(0)
    target_z(0)
    hidden_y(0, 1)
    hidden_y(0, 3)
    product(0, 2)
    hidden_y(0, 2)
    stats_z(0)
    target_z(1)
    product(1, 1)
    stats_core(1)
    product(1, 3)
    stats_y(1)
    hidden_y(1, 1)
    hidden_y(1, 3)
    product(1, 2)
    hidden_y(1, 2)
    loss0 = stats_end(0)
    product(1, 0)
    stats_z(1)
    hidden_z(0)
    loss1 = stats_end(1)
    hidden_z(1)
    gradient(0)
    gradient(1)
    loss[...] = (loss0 + loss1) * (1.0 / 128.0)

    def head_tile(n, _):
        rows = pl.ds(pl.multiple_of(n * 512, 512), 512)
        out = lax.dot_general(
            h[:, rows], grad[...], (((0,), (0,)), ((), ())), preferred_element_type=F32
        )
        head[rows, :] = out.astype(BF16)
        return 0

    lax.fori_loop(0, FEAT // 512, head_tile, 0)
    target_end(0)
    target_end(1)
    hidden_x(0)
    hidden_x(1)
    x_in[x] = x_out[x]
    for d in range(1, NX):
        send(x_out.at[(x + d) % NX], x_in.at[x], gx_s, gx_r, x_peer(d))
    got(x_in.at[pl.ds(0, NX - 1)], gx_r)
    hs32[...] = x_in[...].astype(F32)
    for xx in range(NX):
        for k in range(SUB):
            at0 = xx * FEAT + k * LANES
            ghid[0, :, at0 : at0 + LANES] = hs32[xx, :, k, :].astype(BF16)

    got(hs.at[pl.ds(0, 3)], hx_s)
    got(tx.at[pl.ds(0, 3)], tx_s)
    got(g.at[:, 0, :, 0, pl.ds(0, NZ - 1)], hz_s)
    got(g.at[:, pl.ds(0, NY - 1), :, 0], hy_s)
    got(g.at[:, :, :, 0], hc_s)
    got(relay, rl_s)
    got(final, fn_s)
    got(u.at[:, :, pl.ds(0, NX - 1)], ux_s)
    got(st_core, sc_s)
    got(st_y.at[:, pl.ds(0, NY - 1)], sy_s)
    got(st_z.at[:, pl.ds(0, NZ - 1)], sz_s)
    got(st_raw.at[:, pl.ds(0, NX - 1)], sx_s)
    got(tcore_in, tc_s)
    got(ty_in, ty_s)
    got(tz_in.at[:, pl.ds(0, NZ - 1)], tz_s)
    got(core_in, gc_s)
    got(y_in, gy_s)
    got(z_in.at[:, pl.ds(0, NZ - 1)], gz_s)
    got(x_in.at[pl.ds(0, NX - 1)], gx_s)


def on_device(hidden, out_head, targets, scale_index):
    vmem = pltpu.VMEM
    dma = pltpu.SemaphoreType.DMA
    scratch = [
        vmem((1, 2, NX * FEAT), BF16),
        vmem((1, LANES), jnp.int32),
        vmem((FEAT, WIDTH), BF16),
        vmem((WIDTH, FEAT), BF16),
        vmem((NX, 2, SUB, LANES), F32),
        vmem((NX, 2, SUB, LANES), BF16),
        vmem((2, NY, NX, 2, NZ, SUB, LANES), BF16),
        vmem((CHUNK * SUB, LANES), F32),
        vmem((2 * PART, FEAT), BF16),
        vmem((2 * NY, NX, GROUP, WIDTH), F32),
        vmem((2 * NY, 2, GROUP, HALF), F32),
        vmem((2 * NY, 2, GROUP, WIDTH), F32),
        vmem((2, NY, NX, GROUP, WIDTH), BF16),
        vmem((2 * PART, WIDTH), BF16),
        vmem((PART, WIDTH), BF16),
        vmem((2, 2, NY, NX * NZ, FEAT), BF16),
        vmem((NX, 8, LANES), F32),
        vmem((2, NX, 8, LANES), F32),
        vmem((2, 3, 8, LANES), F32),
        vmem((2, 8, LANES), F32),
        vmem((2, NY, 8, LANES), F32),
        vmem((2, NZ, 8, LANES), F32),
        vmem((2, 8, LANES), F32),
        vmem((2, NY, NX * NZ, FEAT), BF16),
        vmem((2, NY, NX * NZ, FEAT), BF16),
        vmem((2, 2, NY, NX * NZ, FEAT), F32),
        vmem((2, NY - 1, NX * NZ, FEAT), BF16),
        vmem((2, NY - 1, NX * NZ, FEAT), BF16),
        vmem((2, NX, NZ, SUB, LANES), BF16),
        vmem((2, NZ, NX, SUB, LANES), BF16),
        vmem((NX, 2, SUB, LANES), BF16),
        vmem((NX, 2, SUB, LANES), BF16),
        vmem((2, NY, NX * NZ, FEAT), BF16),
        vmem((2, NY - 1, NX * NZ, FEAT), BF16),
        vmem((2, NY - 1, NX * NZ, FEAT), BF16),
        vmem((2, NX, NZ, SUB, LANES), BF16),
        vmem((2, NZ, NX, SUB, LANES), BF16),
        dma, dma, dma, dma, dma, dma((2,)), dma((2, 3)), dma((2, 4)), dma((8, 2)), dma((8, 2)), dma((2, 4)),
        dma((2,)), dma((2,)), dma((2,)), dma((2,)), dma((2, 4)), dma((2,)), dma((2,)), dma,
    ] + [dma] * 16 + [dma((2,))] * 3 + [dma] * 3
    in_hbm = pl.BlockSpec(memory_space=pltpu.HBM)
    in_vmem = pl.BlockSpec(memory_space=pltpu.VMEM)
    head, ghid, loss = pl.pallas_call(
        kernel,
        out_shape=(
            jax.ShapeDtypeStruct((FEAT, WIDTH), BF16),
            jax.ShapeDtypeStruct(hidden.shape, BF16),
            jax.ShapeDtypeStruct((1, 1), F32),
        ),
        in_specs=[
            in_hbm,
            in_hbm,
            in_hbm,
            pl.BlockSpec(memory_space=pltpu.SMEM),
        ],
        out_specs=(in_vmem, in_vmem, in_vmem),
        scratch_shapes=scratch,
        compiler_params=pltpu.CompilerParams(
            collective_id=0, has_side_effects=True, vmem_limit_bytes=VMEM_MIB * 2**20
        ),
    )(hidden, out_head, targets, scale_index)
    return head, ghid, loss.reshape(1)


def solution(mesh):
    in_specs = (
        P("section", "vocab", None),
        P("section", "vocab"),
        P("section", None),
        P("section"),
    )
    out_specs = (P("section", "vocab"), P("section", "vocab", None), P("section"))
    return jax.shard_map(
        on_device, mesh=mesh, in_specs=in_specs, out_specs=out_specs, check_vma=False
    )
```

time: 97.4 us -> 80.1 us (0.82)
  Pallas kernels: 89.9 us -> 72.8 us
    pallas_call x1, Pallas kernels: 89.9 us -> 72.8 us  [on_device(): pl.pallas_call(kernel, out_shape=(jax.ShapeDtypeStruct((FEAT, WIDTH), BF1...]
where the time goes in v3:
time: 80.1 us; the launch traced here: 79.9 us
  Pallas kernels  72.8 us (91%)
  local copies, waits for them, and re-layouts  4.04 us (5%)
  between operations  3.06 us (4%)
    pallas_call x1, Pallas kernels, on_device(): pl.pallas_call(kernel, out_shape=(jax.ShapeDtypeStruct((FEAT, WIDTH), BF1...  72.8 us
    unnamed x6, local copies, waits for them, and re-layouts  4.04 us

profile of v3, /device:TPU:2, one launch (start us, length us, event | category | flops | bytes accessed | tf_op | source)
XLA Modules:
  0.0 79.9 jit_solution(6671193072625507905)
XLA Ops:
  1.3 0.0 copy-start
  1.3 0.7 copy-done
  2.0 0.0 copy-start.1
  2.0 0.7 copy-done.1
  2.7 72.8 %shard_map.67 = (bf16[2048,1024]{1,0:T(8,128)(2,1)S(1)}, bf16[1,2,8192]{2,1,0:T(2,128)(2,1)S(1)}, f32[1,1]{1,0:T(1,128)}) custom-call(bf16[1,2,8192]{2,1,0:T(2,128)(2,1)S(1)} %copy-done, bf16[2048,1024]{1,0:T(8,128)(2,1)} %w_hbm.1, s32[1,128]{1,0:T(1,128)S(1)} %copy-done.1, s32[1]{0:T(128)S(6)} %copy.10.scale), custom_call_target="tpu_custom_call" | custom-call | tf_op jit(solution)/shard_map/pallas_call | solution.py:539
  75.5 2.0 %copy.11 = bf16[2048,1024]{1,0:T(8,128)(2,1)} copy(bf16[2048,1024]{1,0:T(8,128)(2,1)S(1)} %get-tuple-element.12) | data formatting | bytes 8388608
  77.5 0.6 copy.12
Async XLA Ops:
  1.3 0.8 copy-start
  2.0 0.7 copy-start.1

commit v4 on v3

--- a/solution.py
+++ b/solution.py
@@ -313,10 +313,10 @@
     def hidden_z(l):
         got(core_in.at[l, y], gc_r.at[l, 0])
         got(y_in.at[l], gy_r.at[l])
-        lse, weights = st_end[l, 4:6, :], st_end[l, 6:8, :]
-        acc = own_column(weights * jnp.exp(st_y[l, y, 0:2, :] - lse), y) * chip_sum(l, y)
+        peak = st_own[l, 2, 0:2, :]
+        acc = own_column(jnp.exp(st_y[l, y, 0:2, :] - peak), y) * chip_sum(l, y)
         for d in range(1, NY):
-            factor = own_column(weights * jnp.exp(st_y[l, (y + d) % NY, 0:2, :] - lse), y)
+            factor = own_column(jnp.exp(st_y[l, (y + d) % NY, 0:2, :] - peak), y)
             acc = acc + factor * y_in[l, d - 1].astype(F32)
         as_tiles(acc, z_out.at[l])
         z_in[l, z] = z_out[l, :, z]
@@ -325,18 +325,23 @@
 
     def hidden_x(l):
         got(z_in.at[l, pl.ds(0, NZ - 1)], gz_r.at[l])
-        acc = z_in[l, 0].astype(F32)
-        for i in range(1, NZ):
-            acc = acc + z_in[l, i].astype(F32)
-        at_target = tz_in[l, 0].astype(F32)
-        for i in range(1, NZ):
-            at_target = at_target + tz_in[l, i].astype(F32)
         line_at = lax.broadcasted_iota(jnp.int32, (1, LANES), 1)
+
+        def of_row(lines, s):
+            here = line_at == (s % 2) * 64 + y * GROUP + c * NZ + z
+            return jnp.sum(jnp.where(here, lines[s // 2 : s // 2 + 1], 0.0), axis=1, keepdims=True)
+
+        entries = st_end[l, 2:4, :]
+        sums = [jnp.zeros((SUB, LANES), F32)] * NX
+        for i in range(NZ):
+            lines = st_end[l, 6:8, :] * jnp.exp(st_z[l, i, 0:2, :] - st_end[l, 4:6, :])
+            for s in range(NX):
+                sums[s] = sums[s] + of_row(lines, s) * z_in[l, i, s].astype(F32)
         for s in range(NX):
-            here = line_at == (s % 2) * 64 + y * GROUP + c * NZ + z
-            line = st_end[l, 2 + s // 2 : 3 + s // 2, :]
-            entry = jnp.sum(jnp.where(here, line, 0.0), axis=1, keepdims=True)
-            x_out[s, l] = (acc[s] + entry * at_target[s]).astype(BF16)
+            at_target = tz_in[l, 0, s].astype(F32)
+            for i in range(1, NZ):
+                at_target = at_target + tz_in[l, i, s].astype(F32)
+            x_out[s, l] = (sums[s] + of_row(entries, s) * at_target).astype(BF16)
 
     def target_core(l):
         send(hot_w.at[l, oc], tcore_in.at[l], tc_s, tc_r.at[l], core_peer)
@@ -383,10 +388,10 @@
     logits_part(0, 3)
     gathered_y(0, 2)
     target_core(1)
+    softmax_part(0, 0)
+    raised_out(0, 0)
     logits_part(0, 2)
     target_y(0)
-    softmax_part(0, 0)
-    raised_out(0, 0)
     gathered_y(1, 1)
     logits_relay(0, 1)
     gathered_y(1, 3)
@@ -413,35 +418,35 @@
     product(0, 3)
     softmax_part(1, 1)
     raised_out(1, 1)
+    stats_core(0)
     softmax_part(1, 3)
     raised_out(1, 3)
-    stats_core(0)
+    stats_y(0)
+    hidden_y(0, 1)
+    hidden_y(0, 3)
     softmax_part(1, 2)
     stats_x(1)
     raised_out(1, 2)
     raised_out(1, 0)
-    stats_y(0)
     target_z(0)
-    hidden_y(0, 1)
-    hidden_y(0, 3)
+    target_z(1)
     product(0, 2)
+    product(1, 1)
     hidden_y(0, 2)
-    stats_z(0)
-    target_z(1)
-    product(1, 1)
     stats_core(1)
     product(1, 3)
+    stats_z(0)
     stats_y(1)
     hidden_y(1, 1)
+    product(1, 2)
     hidden_y(1, 3)
-    product(1, 2)
     hidden_y(1, 2)
+    stats_z(1)
     loss0 = stats_end(0)
+    hidden_z(0)
     product(1, 0)
-    stats_z(1)
-    hidden_z(0)
+    hidden_z(1)
     loss1 = stats_end(1)
-    hidden_z(1)
     gradient(0)
     gradient(1)
     loss[...] = (loss0 + loss1) * (1.0 / 128.0)
@@ -534,6 +539,7 @@
         dma, dma, dma, dma, dma, dma((2,)), dma((2, 3)), dma((2, 4)), dma((8, 2)), dma((8, 2)), dma((2, 4)),
         dma((2,)), dma((2,)), dma((2,)), dma((2,)), dma((2, 4)), dma((2,)), dma((2,)), dma,
     ] + [dma] * 16 + [dma((2,))] * 3 + [dma] * 3
+    stay = functools.partial(pltpu.with_memory_space_constraint, memory_space=pltpu.HBM)
     in_hbm = pl.BlockSpec(memory_space=pltpu.HBM)
     in_vmem = pl.BlockSpec(memory_space=pltpu.VMEM)
     head, ghid, loss = pl.pallas_call(
@@ -554,7 +560,7 @@
         compiler_params=pltpu.CompilerParams(
             collective_id=0, has_side_effects=True, vmem_limit_bytes=VMEM_MIB * 2**20
         ),
-    )(hidden, out_head, targets, scale_index)
+    )(stay(hidden), out_head, stay(targets), scale_index)
     return head, ghid, loss.reshape(1)
 
 

time: 80.1 us -> 77.9 us (0.973)
  local copies, waits for them, and re-layouts: 4.04 us -> 2.63 us
  Pallas kernels: 72.8 us -> 71.9 us
    unnamed x6 -> x2, local copies, waits for them, and re-layouts: 4.04 us -> 2.63 us
    pallas_call x1, Pallas kernels: 72.8 us -> 71.9 us  [on_device(): pl.pallas_call(kernel, out_shape=(jax.ShapeDtypeStruct((FEAT, WIDTH), BF1...]
where the time goes in v4:
time: 77.9 us; the launch traced here: 77.5 us
  Pallas kernels  71.9 us (92%)
  between operations  2.98 us (4%)
  local copies, waits for them, and re-layouts  2.63 us (3%)
    pallas_call x1, Pallas kernels, on_device(): pl.pallas_call(kernel, out_shape=(jax.ShapeDtypeStruct((FEAT, WIDTH), BF1...  71.9 us
    unnamed x2, local copies, waits for them, and re-layouts  2.63 us

profile of v4, /device:TPU:2, one launch (start us, length us, event | category | flops | bytes accessed | tf_op | source)
XLA Modules:
  0.0 77.5 jit_solution(1062993446356749849)
XLA Ops:
  1.3 71.9 %shard_map.67 = (bf16[2048,1024]{1,0:T(8,128)(2,1)S(1)}, bf16[1,2,8192]{2,1,0:T(2,128)(2,1)S(1)}, f32[1,1]{1,0:T(1,128)}) custom-call(bf16[1,2,8192]{2,1,0:T(2,128)(2,1)} %hid_hbm.1, bf16[2048,1024]{1,0:T(8,128)(2,1)} %w_hbm.1, s32[1,128]{1,0:T(1,128)} %tgt_hbm.1, s32[1]{0:T(128)S(6)} %copy.10.scale), custom_call_target="tpu_custom_call" | custom-call | tf_op jit(solution)/shard_map/pallas_call | solution.py:545
  73.2 2.0 %copy.11 = bf16[2048,1024]{1,0:T(8,128)(2,1)} copy(bf16[2048,1024]{1,0:T(8,128)(2,1)S(1)} %get-tuple-element.12) | data formatting | bytes 8388608
  75.2 0.6 copy.12

commit v5 on v4

--- a/solution.py
+++ b/solution.py
@@ -33,7 +33,7 @@
     hid_sem, tgt_sem, w_sem, hx_r, tx_r, hz_r, hy_r, hc_r, rl_r, fn_r, ux_r,
     sc_r, sy_r, sz_r, sx_r, gc_r, gy_r, gz_r, gx_r,
     hx_s, tx_s, hz_s, hy_s, hc_s, rl_s, fn_s, ux_s,
-    sc_s, sy_s, sz_s, sx_s, gc_s, gy_s, gz_s, gx_s, tc_r, ty_r, tz_r, tc_s, ty_s, tz_s,
+    st_s, gc_s, gy_s, gz_s, gx_s, tc_r, ty_r, tz_r, tc_s, ty_s, tz_s,
 ):
     x = lax.axis_index("section")
     v = lax.axis_index("vocab")
@@ -185,23 +185,21 @@
         out = jnp.dot(h[rows, :], w[...], preferred_element_type=F32)
         part[k] = out.reshape(NX, GROUP, WIDTH)
         far = part.at[k, (x + 2) % NX]
-        send(far.at[:, pl.ds(0, HALF)], relay.at[k, 0], rl_s, rl_r.at[k, 0], x_peer(1))
-        send(far.at[:, pl.ds(HALF, HALF)], relay.at[k, 1], rl_s, rl_r.at[k, 1], x_peer(3))
+        send(far.at[:, pl.ds(0, HALF)], relay.at[k, 0], rl_s, rl_r.at[k], x_peer(1))
+        send(far.at[:, pl.ds(HALF, HALF)], relay.at[k, 1], rl_s, rl_r.at[k], x_peer(3))
 
     def logits_relay(l, d):
         k = l * NY + d
         right, left = (x + 1) % NX, (x + 3) % NX
-        got(relay.at[k, 0], rl_r.at[k, 0])
+        got(relay.at[k], rl_r.at[k])
         part[k, right, :, :HALF] = part[k, right, :, :HALF] + relay[k, 0]
-        send(part.at[k, right], final.at[k, 0], fn_s, fn_r.at[k, 0], x_peer(1))
-        got(relay.at[k, 1], rl_r.at[k, 1])
+        send(part.at[k, right], final.at[k, 0], fn_s, fn_r.at[k], x_peer(1))
         part[k, left, :, HALF:] = part[k, left, :, HALF:] + relay[k, 1]
-        send(part.at[k, left], final.at[k, 1], fn_s, fn_r.at[k, 1], x_peer(3))
+        send(part.at[k, left], final.at[k, 1], fn_s, fn_r.at[k], x_peer(3))
 
     def softmax_part(l, d):
         py, k = from_y(d), l * NY + d
-        got(final.at[k, 0], fn_r.at[k, 0])
-        got(final.at[k, 1], fn_r.at[k, 1])
+        got(final.at[k], fn_r.at[k])
         logits = part[k, x] + final[k, 0] + final[k, 1]
         peak = jnp.max(logits, axis=1, keepdims=True)
         raised = jnp.exp(logits - peak)
@@ -233,26 +231,26 @@
 
     def stats_x(l):
         for d in range(1, NX):
-            send(st_raw.at[l, x], st_raw.at[l, x], sx_s, sx_r.at[l], x_peer(d))
+            send(st_raw.at[l, x], st_raw.at[l, x], st_s, sx_r.at[l], x_peer(d))
 
     def stats_core(l):
         got(st_raw.at[l, pl.ds(0, NX - 1)], sx_r.at[l])
         st_own[l, 0] = st_raw[l, 0] + st_raw[l, 1] + st_raw[l, 2] + st_raw[l, 3]
-        send(st_own.at[l, 0], st_core.at[l], sc_s, sc_r.at[l], core_peer)
+        send(st_own.at[l, 0], st_core.at[l], st_s, sc_r.at[l], core_peer)
 
     def stats_y(l):
         got(st_core.at[l], sc_r.at[l])
         put(st_own.at[l, 1], merged([st_own[l, 0], st_core[l]]))
         st_y[l, y] = st_own[l, 1]
         for d in range(1, NY):
-            send(st_own.at[l, 1], st_y.at[l, y], sy_s, sy_r.at[l], y_peer(d))
+            send(st_own.at[l, 1], st_y.at[l, y], st_s, sy_r.at[l], y_peer(d))
 
     def stats_z(l):
         got(st_y.at[l, pl.ds(0, NY - 1)], sy_r.at[l])
         put(st_own.at[l, 2], merged([st_y[l, i] for i in range(NY)]))
         st_z[l, z] = st_own[l, 2]
         for d in Z_ORDER:
-            send(st_own.at[l, 2], st_z.at[l, z], sz_s, sz_r.at[l], z_peer(d))
+            send(st_own.at[l, 2], st_z.at[l, z], st_s, sz_r.at[l], z_peer(d))
 
     def stats_end(l):
         got(st_z.at[l, pl.ds(0, NZ - 1)], sz_r.at[l])
@@ -482,10 +480,7 @@
     got(relay, rl_s)
     got(final, fn_s)
     got(u.at[:, :, pl.ds(0, NX - 1)], ux_s)
-    got(st_core, sc_s)
-    got(st_y.at[:, pl.ds(0, NY - 1)], sy_s)
-    got(st_z.at[:, pl.ds(0, NZ - 1)], sz_s)
-    got(st_raw.at[:, pl.ds(0, NX - 1)], sx_s)
+    got(f.at[pl.ds(0, 28 * 8)], st_s)
     got(tcore_in, tc_s)
     got(ty_in, ty_s)
     got(tz_in.at[:, pl.ds(0, NZ - 1)], tz_s)
@@ -536,9 +531,9 @@
         vmem((2, NY - 1, NX * NZ, FEAT), BF16),
         vmem((2, NX, NZ, SUB, LANES), BF16),
         vmem((2, NZ, NX, SUB, LANES), BF16),
-        dma, dma, dma, dma, dma, dma((2,)), dma((2, 3)), dma((2, 4)), dma((8, 2)), dma((8, 2)), dma((2, 4)),
+        dma, dma, dma, dma, dma, dma((2,)), dma((2, 3)), dma((2, 4)), dma((8,)), dma((8,)), dma((2, 4)),
         dma((2,)), dma((2,)), dma((2,)), dma((2,)), dma((2, 4)), dma((2,)), dma((2,)), dma,
-    ] + [dma] * 16 + [dma((2,))] * 3 + [dma] * 3
+    ] + [dma] * 13 + [dma((2,))] * 3 + [dma] * 3
     stay = functools.partial(pltpu.with_memory_space_constraint, memory_space=pltpu.HBM)
     in_hbm = pl.BlockSpec(memory_space=pltpu.HBM)
     in_vmem = pl.BlockSpec(memory_space=pltpu.VMEM)

time: 77.9 us -> 77.4 us (level)
  no operation moved by 1% of the time
where the time goes in v5:
time: 77.4 us; the launch traced here: 77.2 us
  Pallas kernels  71.6 us (93%)
  between operations  2.98 us (4%)
  local copies, waits for them, and re-layouts  2.63 us (3%)
    pallas_call x1, Pallas kernels, on_device(): pl.pallas_call(kernel, out_shape=(jax.ShapeDtypeStruct((FEAT, WIDTH), BF1...  71.6 us
    unnamed x2, local copies, waits for them, and re-layouts  2.63 us

profile of v5, /device:TPU:2, one launch (start us, length us, event | category | flops | bytes accessed | tf_op | source)
XLA Modules:
  0.0 77.2 jit_solution(11648400161073581556)
XLA Ops:
  1.3 71.6 %shard_map.67 = (bf16[2048,1024]{1,0:T(8,128)(2,1)S(1)}, bf16[1,2,8192]{2,1,0:T(2,128)(2,1)S(1)}, f32[1,1]{1,0:T(1,128)}) custom-call(bf16[1,2,8192]{2,1,0:T(2,128)(2,1)} %hid_hbm.1, bf16[2048,1024]{1,0:T(8,128)(2,1)} %w_hbm.1, s32[1,128]{1,0:T(1,128)} %tgt_hbm.1, s32[1]{0:T(128)S(6)} %copy.10.scale), custom_call_target="tpu_custom_call" | custom-call | tf_op jit(solution)/shard_map/pallas_call | solution.py:540
  72.8 2.0 %copy.11 = bf16[2048,1024]{1,0:T(8,128)(2,1)} copy(bf16[2048,1024]{1,0:T(8,128)(2,1)S(1)} %get-tuple-element.12) | data formatting | bytes 8388608
  74.9 0.6 copy.12
